TPU v7x, 32 devices: a whole 2x2x4 slice. The times are simulated.
32 devices in a mesh: groups: 2 (over y), tile: 16 (over z, x, core).
Axes of the slice: x: 2, y: 2, z: 4, core: 2. Of those that a mesh axis runs over, the one named last changes fastest.
Arguments:
- rhs: float32 [4096, 320], P(('groups', 'tile')), parts along dimension 0, may hold values from -8 to 8
- counts: int32 [32], P('groups'), parts along dimension 0, may hold values from 32 to 128, as said below
- local_target: int32 [4096, 24], P(('groups', 'tile')), parts along dimension 0, may hold values from 0 to 127
- local_offset: int32 [4096, 24], P(('groups', 'tile')), parts along dimension 0, may hold values from 0 to 31
- remote_tile: int32 [4096, 4], P(('groups', 'tile')), parts along dimension 0, may hold values from 0 to 15, all different within a row; in each aligned block of 128 rows (0 to 127, 128 to 255, ...) at most 64 rows name the same one
- remote_target: int32 [4096, 4], P(('groups', 'tile')), parts along dimension 0, may hold values from 0 to 127
- remote_offset: int32 [4096, 4], P(('groups', 'tile')), parts along dimension 0, may hold values from 0 to 31
- lattice: bfloat16 [32, 320, 320], replicated, may hold values from -2 to 2
- tmatrix: bfloat16 [320, 320], replicated, may hold values from -1 to 1
Outputs:
- basis: float32 [4, 4096, 320], P(None, ('groups', 'tile')), parts along dimension 1
- hess: float32 [8, 3], P('groups'), parts along dimension 0
There are 2 independent parts, one for each index of `groups`. A program takes and returns all parts, laid end to end along the dimension named above; an argument that names none is the same for every part. Nothing has to cross between parts.
Inputs may be any that keep to these rules, and one draw needn't show every extreme that they name: counts[t] is a tile's live clusters; some tile has all 128 slots live. `remote_tile`: each cluster names 4 different tiles; among the clusters of one tile, no tile is named more than 64 times.
All inputs are finite; a program needn't handle non-finite values.
Results may differ from a plain program's by a relative error of at most 0.0048.
Values may be sent and summed in bfloat16 or wider, within the bound.
No kernel may reach another device: no remote copies, remote signals or barrier semaphores. Data moves between devices by JAX's collectives and lax.ppermute only.
A program may use at most 64 MiB of HBM per device.

v0:
```python
import jax
import jax.numpy as jnp
from jax import lax
from jax.sharding import PartitionSpec as P

ITERS = 3


def norm_of(vector):
    return jnp.sqrt(lax.psum(jnp.sum(vector * vector), "tile"))


def per_device(
    rhs,
    counts,
    local_target,
    local_offset,
    remote_tile,
    remote_target,
    remote_offset,
    lattice,
    tmatrix,
):
    tiles = lax.axis_size("tile")
    mine = lax.axis_index("tile")
    cap, width = rhs.shape
    nl = local_target.shape[1]
    nr = remote_tile.shape[1]
    noff = lattice.shape[0]
    steps_total = ITERS
    send_cap = max(2, 2 * cap * nr // tiles)
    dump = cap * noff
    own_count = counts[mine]
    live = (jnp.arange(cap, dtype=jnp.int32) < own_count).astype(jnp.float32)
    start = rhs * live[:, None]
    local_code = (local_target % own_count * noff + local_offset).reshape(-1)
    dest = remote_tile.reshape(-1)
    remote_code = (remote_target % counts[remote_tile] * noff + remote_offset).reshape(-1)
    onehot = (dest[:, None] == jnp.arange(tiles, dtype=jnp.int32)[None, :]).astype(jnp.int32)
    rank = jnp.sum((jnp.cumsum(onehot, axis=0) - onehot) * onehot, axis=1)
    slot_index = dest * send_cap + rank
    source = jnp.arange(cap * nr, dtype=jnp.int32) // nr
    inverse = jnp.full((tiles * send_cap,), cap, jnp.int32).at[slot_index].set(source)
    codes_out = (
        jnp.full((tiles * send_cap,), dump, jnp.int32)
        .at[slot_index]
        .set(remote_code)
        .reshape(tiles, send_cap)
    )
    lattice_flat = lattice.reshape(noff * width, width)
    vectors = [start / norm_of(start)]
    hess = jnp.zeros((steps_total + 1, steps_total), jnp.float32)
    for step in range(steps_total):
        vector = vectors[step]
        xb = vector.astype(jnp.bfloat16)
        padded = jnp.concatenate([xb, jnp.zeros((1, width), jnp.bfloat16)])
        rows_out = padded[inverse].reshape(tiles, send_cap, width)
        rows_in = lax.all_to_all(rows_out, "tile", split_axis=0, concat_axis=0, tiled=True)
        codes_in = lax.all_to_all(codes_out, "tile", split_axis=0, concat_axis=0, tiled=True)
        rows = jnp.concatenate([jnp.repeat(xb, nl, axis=0), rows_in.reshape(-1, width)]).astype(
            jnp.float32
        )
        codes = jnp.concatenate([local_code, codes_in.reshape(-1)])
        summed = jax.ops.segment_sum(rows, codes, num_segments=dump + 1)
        summed = summed[:dump].reshape(cap, noff * width).astype(jnp.bfloat16)
        field = jnp.dot(summed, lattice_flat, preferred_element_type=jnp.float32).astype(
            jnp.bfloat16
        )
        scattered = jnp.dot(field, tmatrix, preferred_element_type=jnp.float32)
        image = vector - live[:, None] * scattered
        for j in range(step + 1):
            product = lax.psum(jnp.sum(vectors[j] * image), "tile")
            image = image - product * vectors[j]
            hess = hess.at[j, step].set(product)
        length = norm_of(image)
        hess = hess.at[step + 1, step].set(length)
        vectors.append(image / length)
    return (jnp.stack(vectors), hess)


def solution(mesh):
    placed = (
        P(("groups", "tile"), None),
        P("groups"),
        P(("groups", "tile"), None),
        P(("groups", "tile"), None),
        P(("groups", "tile"), None),
        P(("groups", "tile"), None),
        P(("groups", "tile"), None),
        P(),
        P(),
    )
    return jax.shard_map(
        per_device,
        mesh=mesh,
        in_specs=placed,
        out_specs=(P(None, ("groups", "tile"), None), P("groups", None)),
        check_vma=False,
    )
```

profile of v0, /device:TPU:0, one launch (start us, length us, event | category | flops | bytes accessed | tf_op | source)
XLA Modules:
  0.0 591.5 jit_solution(4700499930087989121)
XLA Ops:
  0.7 0.8 copy.19
  1.7 2.0 fusion.44
  3.7 10.9 %fusion.29 = (s32[128,4]{0,1:T(4,128)S(1)}, s32[128,4]{0,1:T(4,128)S(1)}) fusion(s32[128,4]{0,1:T(4,128)} %param.33, s32[128,4]{0,1:T(4,128)} %param.32, s32[128,4]{0,1:T(4,128)} %param.31, s32[]{:T(128)} %bitcast.5, s32[]{:T(128)} %bitcast.6, s32[]{:T(128)} %bitcast.7, s32[]{:T(128)} %bitcast.8, s32[]{:T(128)} %bitcast.9, s32[]{:T(128)} %bitcast.10, ...), kind=kLoop, calls=%fused_computation.83 | loop fusion | flops 23552 | bytes 10304 | tf_op jit(solution)/shard_map/add | solution.py:38
  14.8 1.2 reduce-window.6
  16.6 2.4 scatter_custom_fusion
  19.0 0.7 all_to_all.17
  19.7 7.4 %all-to-all-start = ((s32[16,1,64]{2,1,0:T(1,128)}), s32[16,1,64]{2,1,0:T(1,128)S(1)}, u32[]{:S(2)}, u32[]{:S(2)}) async-start(s32[16,1,64]{2,1,0:T(1,128)} %all_to_all.17), calls=%async_computation | async-start | bytes 16384 | tf_op jit(solution)/shard_map/all_to_all | solution.py:59
  27.1 0.6 compare_convert_fusion
  27.6 1.6 multiply_reduce_fusion.9
  29.2 34.5 %psum.70 = f32[]{:T(128)} all-reduce(f32[]{:T(128)} %multiply_reduce_fusion.9), channel_id=1, replica_groups=mesh['groups'=2,'tile'=16] {'tile'}, use_global_device_ids=true, to_apply=%region_1.2 | all-reduce | flops 1 | bytes 8 | tf_op jit(solution)/shard_map/psum | solution.py:10
  64.4 1.6 fusion.40
  66.0 2.4 scatter_custom_fusion.1
  68.6 5.0 gather_fusion
  73.6 3.6 all-to-all-start.1
  79.2 0.7 reduce.29
  79.9 15.9 %all-to-all-done.1 = bf16[16,64,320]{2,1,0:T(8,128)(2,1)S(1)} async-done(((bf16[16,64,320]{2,1,0:T(8,128)(2,1)}), bf16[16,64,320]{2,1,0:T(8,128)(2,1)S(1)}, u32[]{:S(2)}, u32[]{:S(2)}) %all-to-all-start.1) | async-done | bytes 655392 | tf_op jit(solution)/shard_map/all_to_all | solution.py:58
  96.1 31.6 %scatter_custom_fusion.2 = f32[4097,320]{1,0:T(8,128)} fusion(s32[4096]{0:T(1024)S(1)} %constant_dynamic-update-slice_fusion, f32[]{:T(128)} %constant.283.clone.1, bf16[1024,320]{1,0:T(8,128)(2,1)S(1)} %bitcast.87, bf16[]{:T(256)} %constant.325, bf16[3072,320]{1,0:T(8,128)(2,1)S(1)} %bitcast.82), kind=kCustom, calls=%fused_computation.15 | custom fusion | flops 6553600 | bytes 8389894 | tf_op jit(solution)/shard_map/scatter-add | solution.py:64
  127.7 3.2 slice.229
  130.9 4.2 convert_element_type.58
  135.1 6.3 %multiply_reduce_fusion.8 = (f32[]{:T(128)}, f32[128,320]{0,1:T(8,128)S(1)}) fusion(f32[]{:T(128)S(6)} %sqrt.12, f32[128,320]{0,1:T(8,128)S(1)} %copy-done.1, f32[128]{0:T(128)} %copy-done.12, bf16[320,320]{1,0:T(8,128)(2,1)S(1)} %copy-done, bf16[128,10240]{1,0:T(8,128)(2,1)} %convert_element_type.58, bf16[10240,320]{1,0:T(8,128)(2,1)} %bitcast.78), kind=kOutput, calls=%fused_computation.54 | convolution fusion | flops 865361920 | bytes 9708040 | tf_op jit(solution)/shard_map/dot_general | solution.py:69
  141.4 33.7 %psum.71 = f32[]{:T(128)} all-reduce(f32[]{:T(128)} %get-tuple-element.142), channel_id=1, replica_groups=mesh['groups'=2,'tile'=16] {'tile'}, use_global_device_ids=true, to_apply=%region_9.10 | all-reduce | flops 1 | bytes 8 | tf_op jit(solution)/shard_map/psum | solution.py:72
  175.1 1.4 multiply_reduce_fusion.7
  176.5 30.2 %psum.72 = f32[]{:T(128)} all-reduce(f32[]{:T(128)} %multiply_reduce_fusion.7), channel_id=1, replica_groups=mesh['groups'=2,'tile'=16] {'tile'}, use_global_device_ids=true, to_apply=%region_11.12 | all-reduce | flops 1 | bytes 8 | tf_op jit(solution)/shard_map/psum | solution.py:10
  207.4 1.4 fusion.41
  208.9 0.6 copy-done.7
  209.6 3.9 gather_fusion.1
  213.5 22.8 %all_to_all.26 = bf16[16,64,320]{2,1,0:T(8,128)(2,1)S(1)} all-to-all(bf16[16,64,320]{2,1,0:T(8,128)(2,1)S(1)} %bitcast.85), channel_id=1, replica_groups=mesh['groups'=2,'tile'=16] {'tile'}, dimensions={0} | all-to-all | bytes 1310720 | tf_op jit(solution)/shard_map/all_to_all | solution.py:58
  236.3 1.1 broadcast_in_dim.46
  237.4 31.8 %scatter_custom_fusion.3 = f32[4097,320]{1,0:T(8,128)} fusion(s32[4096]{0:T(1024)} %copy-done.18, f32[]{:T(128)} %constant.283.clone.1, bf16[1024,320]{1,0:T(8,128)(2,1)S(1)} %bitcast.88, bf16[]{:T(256)} %constant.325, bf16[3072,320]{1,0:T(8,128)(2,1)S(1)} %bitcast.83), kind=kCustom, calls=%fused_computation.13 | custom fusion | flops 6553600 | bytes 7866624 | tf_op jit(solution)/shard_map/scatter-add | solution.py:64
  269.2 3.1 slice.228
  272.3 4.2 convert_element_type.62
  276.5 6.4 %multiply_reduce_fusion.6 = (f32[]{:T(128)}, f32[128,320]{0,1:T(8,128)S(1)}) fusion(f32[]{:T(128)S(6)} %sqrt.12, f32[128,320]{0,1:T(8,128)S(1)} %copy-done.1, f32[128]{0:T(128)} %copy-done.12, f32[128,320]{0,1:T(8,128)} %get-tuple-element.115, bf16[320,320]{1,0:T(8,128)(2,1)S(1)} %copy-done, bf16[128,10240]{1,0:T(8,128)(2,1)} %convert_element_type.62, ...), kind=kOutput, calls=%fused_computation.51 | convolution fusion | flops 865361920 | bytes 9871880 | tf_op jit(solution)/shard_map/dot_general | solution.py:69
  282.9 32.1 %psum.73 = f32[]{:T(128)} all-reduce(f32[]{:T(128)} %get-tuple-element.144), channel_id=1, replica_groups=mesh['groups'=2,'tile'=16] {'tile'}, use_global_device_ids=true, to_apply=%region_14.15 | all-reduce | flops 1 | bytes 8 | tf_op jit(solution)/shard_map/psum | solution.py:72
  315.0 1.3 multiply_reduce_fusion.5
  316.3 30.2 %psum.74 = f32[]{:T(128)} all-reduce(f32[]{:T(128)} %multiply_reduce_fusion.5), channel_id=1, replica_groups=mesh['groups'=2,'tile'=16] {'tile'}, use_global_device_ids=true, to_apply=%region_16.17 | all-reduce | flops 1 | bytes 8 | tf_op jit(solution)/shard_map/psum | solution.py:72
  346.5 2.0 multiply_reduce_fusion.4
  348.4 30.4 %psum.75 = f32[]{:T(128)} all-reduce(f32[]{:T(128)} %get-tuple-element.112), channel_id=1, replica_groups=mesh['groups'=2,'tile'=16] {'tile'}, use_global_device_ids=true, to_apply=%region_18.19 | all-reduce | flops 1 | bytes 8 | tf_op jit(solution)/shard_map/psum | solution.py:10
  379.7 5.0 gather_fusion.2
  384.6 3.6 all-to-all-start.3
  388.3 0.6 fusion.43
  388.9 0.6 fusion.42
  389.5 0.7 and_reduce_fusion
  390.2 0.6 scatter.46
  390.9 1.9 scatter.50
  392.8 0.8 scatter.51
  393.7 13.3 %all-to-all-done.3 = bf16[16,64,320]{2,1,0:T(8,128)(2,1)S(1)} async-done(((bf16[16,64,320]{2,1,0:T(8,128)(2,1)}), bf16[16,64,320]{2,1,0:T(8,128)(2,1)S(1)}, u32[]{:S(2)}, u32[]{:S(2)}) %all-to-all-start.3) | async-done | bytes 655392 | tf_op jit(solution)/shard_map/all_to_all | solution.py:58
  406.9 1.1 broadcast_in_dim.47
  408.1 31.8 %scatter_custom_fusion.4 = f32[4097,320]{1,0:T(8,128)} fusion(s32[4096]{0:T(1024)} %copy-done.18, f32[]{:T(128)} %constant.283.clone.1, bf16[1024,320]{1,0:T(8,128)(2,1)S(1)} %bitcast.86, bf16[]{:T(256)} %constant.325, bf16[3072,320]{1,0:T(8,128)(2,1)S(1)} %bitcast.81), kind=kCustom, calls=%fused_computation.11 | custom fusion | flops 6553600 | bytes 7866624 | tf_op jit(solution)/shard_map/scatter-add | solution.py:64
  439.8 3.1 slice.227
  442.9 4.2 convert_element_type.66
  447.2 6.4 %multiply_reduce_fusion.3 = (f32[]{:T(128)}, f32[128,320]{0,1:T(8,128)S(1)}) fusion(f32[]{:T(128)S(6)} %sqrt.12, f32[128,320]{0,1:T(8,128)S(1)} %copy-done.1, f32[128]{0:T(128)} %copy-done.12, bf16[320,320]{1,0:T(8,128)(2,1)S(1)} %copy-done, bf16[128,10240]{1,0:T(8,128)(2,1)} %convert_element_type.66, bf16[10240,320]{1,0:T(8,128)(2,1)} %bitcast.80, ...), kind=kOutput, calls=%fused_computation.46 | convolution fusion | flops 865402880 | bytes 9871884 | tf_op jit(solution)/shard_map/dot_general | solution.py:69
  453.6 33.7 %psum.76 = f32[]{:T(128)} all-reduce(f32[]{:T(128)} %get-tuple-element.146), channel_id=1, replica_groups=mesh['groups'=2,'tile'=16] {'tile'}, use_global_device_ids=true, to_apply=%region_21.22 | all-reduce | flops 1 | bytes 8 | tf_op jit(solution)/shard_map/psum | solution.py:72
  487.3 1.3 multiply_reduce_fusion.2
  488.8 30.0 %psum.77 = f32[]{:T(128)} all-reduce(f32[]{:T(128)} %multiply_reduce_fusion.2), channel_id=1, replica_groups=mesh['groups'=2,'tile'=16] {'tile'}, use_global_device_ids=true, to_apply=%region_23.24 | all-reduce | flops 1 | bytes 8 | tf_op jit(solution)/shard_map/psum | solution.py:72
  518.8 2.0 multiply_reduce_fusion.1
  520.8 30.2 %psum.78 = f32[]{:T(128)} all-reduce(f32[]{:T(128)} %get-tuple-element.110), channel_id=1, replica_groups=mesh['groups'=2,'tile'=16] {'tile'}, use_global_device_ids=true, to_apply=%region_25.26 | all-reduce | flops 1 | bytes 8 | tf_op jit(solution)/shard_map/psum | solution.py:72
  550.9 1.3 multiply_reduce_fusion
  552.3 1.9 dynamic-slice.61
  554.2 30.1 %psum.79 = f32[]{:T(128)} all-reduce(f32[]{:T(128)} %multiply_reduce_fusion), channel_id=1, replica_groups=mesh['groups'=2,'tile'=16] {'tile'}, use_global_device_ids=true, to_apply=%region_27.28 | all-reduce | flops 1 | bytes 8 | tf_op jit(solution)/shard_map/psum | solution.py:10
  584.9 0.7 divide_bitcast_fusion
  587.5 1.4 scatter.66
  588.9 0.8 scatter.67
  589.7 0.8 scatter.68
  590.6 0.9 pad_maximum_fusion
  (80 shorter events, 3.0 us)
Async XLA Ops:
  0.6 134.5 %copy-start = (bf16[320,320]{1,0:T(8,128)(2,1)S(1)}, bf16[320,320]{1,0:T(8,128)(2,1)}, u32[]{:S(2)}) copy-start(bf16[320,320]{1,0:T(8,128)(2,1)} %param.35) | copy-start | bytes 614404
  0.6 77.6 %copy-start.16 = (s32[128,24]{0,1:T(8,128)S(1)}, s32[128,24]{0,1:T(8,128)}, u32[]{:S(2)}) copy-start(s32[128,24]{0,1:T(8,128)} %param.30) | copy-start | bytes 36868
  0.7 77.6 %copy-start.17 = (s32[128,24]{0,1:T(8,128)S(1)}, s32[128,24]{0,1:T(8,128)}, u32[]{:S(2)}) copy-start(s32[128,24]{0,1:T(8,128)} %param.29) | copy-start | bytes 36868
  19.7 53.9 %all-to-all-start = ((s32[16,1,64]{2,1,0:T(1,128)}), s32[16,1,64]{2,1,0:T(1,128)S(1)}, u32[]{:S(2)}, u32[]{:S(2)}) async-start(s32[16,1,64]{2,1,0:T(1,128)} %all_to_all.17), calls=%async_computation | async-start | bytes 16384 | tf_op jit(solution)/shard_map/all_to_all | solution.py:59
  27.6 40.8 %copy-start.12 = (f32[128]{0:T(128)}, f32[128]{0:T(128)S(1)}, u32[]{:S(2)}) copy-start(f32[128]{0:T(128)S(1)} %compare_convert_fusion) | copy-start | bytes 1540
  68.4 27.4 %copy-start.9 = (s32[1024]{0:T(1024)}, s32[1024]{0:T(1024)S(1)}, u32[]{:S(2)}) copy-start(s32[1024]{0:T(1024)S(1)} %fusion.27) | copy-start | bytes 12292
  73.6 22.3 %all-to-all-start.1 = ((bf16[16,64,320]{2,1,0:T(8,128)(2,1)}), bf16[16,64,320]{2,1,0:T(8,128)(2,1)S(1)}, u32[]{:S(2)}, u32[]{:S(2)}) async-start(bf16[16,64,320]{2,1,0:T(8,128)(2,1)} %bitcast.22), calls=%async_computation.1 | async-start | bytes 1572864 | tf_op jit(solution)/shard_map/all_to_all | solution.py:58
  79.9 16.2 %copy-start.18 = (s32[4096]{0:T(1024)}, s32[4096]{0:T(1024)S(1)}, u32[]{:S(2)}) copy-start(s32[4096]{0:T(1024)S(1)} %constant_dynamic-update-slice_fusion) | copy-start | bytes 49156
  127.7 7.4 %copy-start.1 = (f32[128,320]{0,1:T(8,128)S(1)}, f32[128,320]{0,1:T(8,128)}, u32[]{:S(2)}) copy-start(f32[128,320]{0,1:T(8,128)} %param.27) | copy-start | bytes 491524
  135.1 40.0 %copy-start.13 = (f32[128]{0:T(128)S(1)}, f32[128]{0:T(128)}, u32[]{:S(2)}) copy-start(f32[128]{0:T(128)} %copy-done.12) | copy-start | bytes 1540
  135.1 74.5 %copy-start.10 = (s32[1024]{0:T(1024)S(1)}, s32[1024]{0:T(1024)}, u32[]{:S(2)}) copy-start(s32[1024]{0:T(1024)} %copy-done.9) | copy-start | bytes 12292
  208.9 0.6 copy-start.7
  276.5 38.5 %copy-start.2 = (f32[128,320]{0,1:T(8,128)S(1)}, f32[128,320]{0,1:T(8,128)}, u32[]{:S(2)}) copy-start(f32[128,320]{0,1:T(8,128)} %get-tuple-element.115) | copy-start | bytes 491524
  276.5 38.5 %copy-start.14 = (f32[128]{0:T(128)S(1)}, f32[128]{0:T(128)}, u32[]{:S(2)}) copy-start(f32[128]{0:T(128)} %copy-done.12) | copy-start | bytes 1540
  276.5 103.1 %copy-start.11 = (s32[1024]{0:T(1024)S(1)}, s32[1024]{0:T(1024)}, u32[]{:S(2)}) copy-start(s32[1024]{0:T(1024)} %copy-done.9) | copy-start | bytes 12292
  282.9 106.6 %copy-start.22 = (s32[2]{0:T(128)S(1)}, s32[2]{0:T(128)}, u32[]{:S(2)}) copy-start(s32[2]{0:T(128)} %constant.295.clone.1) | copy-start | bytes 28
  348.4 58.5 %copy-start.4 = (f32[128,320]{0,1:T(8,128)}, f32[128,320]{0,1:T(8,128)S(1)}, u32[]{:S(2)}) copy-start(f32[128,320]{0,1:T(8,128)S(1)} %get-tuple-element.113) | copy-start | bytes 491524
  379.6 27.3 %copy-start.6 = (bf16[128,320]{1,0:T(8,128)(2,1)}, bf16[128,320]{1,0:T(8,128)(2,1)S(1)}, u32[]{:S(2)}) copy-start(bf16[128,320]{1,0:T(8,128)(2,1)S(1)} %copy.27) | copy-start | bytes 245764
  384.6 22.3 %all-to-all-start.3 = ((bf16[16,64,320]{2,1,0:T(8,128)(2,1)}), bf16[16,64,320]{2,1,0:T(8,128)(2,1)S(1)}, u32[]{:S(2)}, u32[]{:S(2)}) async-start(bf16[16,64,320]{2,1,0:T(8,128)(2,1)} %bitcast.31), calls=%async_computation.3 | async-start | bytes 1572864 | tf_op jit(solution)/shard_map/all_to_all | solution.py:58
  393.6 13.3 %copy-start.19 = (f32[4,3]{1,0:T(4,128)}, f32[4,3]{1,0:T(4,128)S(1)}, u32[]{:S(2)}) copy-start(f32[4,3]{1,0:T(4,128)S(1)} %scatter.51) | copy-start | bytes 148
  447.1 40.2 %copy-start.3 = (f32[128,320]{0,1:T(8,128)S(1)}, f32[128,320]{0,1:T(8,128)}, u32[]{:S(2)}) copy-start(f32[128,320]{0,1:T(8,128)} %get-tuple-element.115) | copy-start | bytes 491524
  447.1 40.2 %copy-start.15 = (f32[128]{0:T(128)S(1)}, f32[128]{0:T(128)}, u32[]{:S(2)}) copy-start(f32[128]{0:T(128)} %copy-done.12) | copy-start | bytes 1540
  447.1 41.5 %copy-start.20 = (f32[4,3]{1,0:T(4,128)S(1)}, f32[4,3]{1,0:T(4,128)}, u32[]{:S(2)}) copy-start(f32[4,3]{1,0:T(4,128)} %copy-done.19) | copy-start | bytes 148
  447.1 71.6 %copy-start.5 = (f32[128,320]{0,1:T(8,128)S(1)}, f32[128,320]{0,1:T(8,128)}, u32[]{:S(2)}) copy-start(f32[128,320]{0,1:T(8,128)} %copy-done.4) | copy-start | bytes 491524
  447.1 143.5 %copy-start.8 = (f32[1,128,320]{1,2,0:T(8,128)S(1)}, f32[1,128,320]{1,2,0:T(8,128)}, u32[]{:S(2)}) copy-start(f32[1,128,320]{1,2,0:T(8,128)} %get-tuple-element.116) | copy-start | bytes 491524
  590.6 0.9 copy-start.21
where the time goes:
time: 593 us; the launch traced here: 592 us
  blocking collectives  338 us (57%)
  other arithmetic  125 us (21%)
  local copies, waits for them, and re-layouts  59.2 us (10%)
  waiting for transfers between devices  29.2 us (5%)
  matrix products  19.1 us (3%)
  starting transfers between devices  14.6 us (2%)
  between operations  6.84 us (1%)
    psum x6, blocking collectives, per_device(): product = lax.psum(jnp.sum(vectors[j] * image), 'tile')  190 us
    psum x4, blocking collectives, norm_of(): return jnp.sqrt(lax.psum(jnp.sum(vector * vector), 'tile'))  125 us
    scatter-add x3, other arithmetic, per_device(): summed = jax.ops.segment_sum(rows, codes, num_segments=dump + 1)  95.1 us
    all_to_all x2, waiting for transfers between devices, per_device(): lax.all_to_all(rows_out, 'tile', split_axis=0, concat_axis=0, tiled=True)  29.2 us
    all_to_all x1, blocking collectives, per_device(): lax.all_to_all(rows_out, 'tile', split_axis=0, concat_axis=0, tiled=True)  22.8 us
    dot_general x3, matrix products, per_device(): scattered = jnp.dot(field, tmatrix, preferred_element_type=jnp.float32)  19.1 us
    gather x3, local copies, waits for them, and re-layouts, per_device(): rows_out = padded[inverse].reshape(tiles, send_cap, width)  13.8 us
    convert_element_type x3, local copies, waits for them, and re-layouts, per_device(): summed = summed[:dump].reshape(cap, noff * width).astype(jnp.bfloat16)  12.6 us
  transfers between devices with their start and end apart: 3, of which 2 were waited for; matrix products, arithmetic and copies ran while one was open for 3% of the time, Pallas kernels for 0%

commit v1 on v0

v1 whole, which is shorter than its diff:
```python
import functools

import jax
import jax.numpy as jnp
from jax import lax
from jax.experimental import pallas as pl
from jax.experimental.pallas import tpu as pltpu
from jax.sharding import PartitionSpec as P

ITERS = 3
LANES = 128
GROUP = 4
F32 = jnp.float32
BF16 = jnp.bfloat16
VMEM_LIMIT = 56 * 1024 * 1024


def iota(shape, dim):
    return lax.broadcasted_iota(jnp.int32, shape, dim)


def dot(a, b):
    return lax.dot_general(a, b, (((1,), (0,)), ((), ())), preferred_element_type=F32)


def dot_nt(a, b):
    return lax.dot_general(a, b, (((1,), (1,)), ((), ())), preferred_element_type=F32)


def flip(table):
    rows = table.shape[0]
    eye = (iota((rows, rows), 0) == iota((rows, rows), 1)).astype(BF16)
    return lax.dot_general(
        table.astype(F32).astype(BF16), eye, (((0,), (0,)), ((), ())), preferred_element_type=F32
    )


def total(values):
    return jnp.sum(jnp.sum(values, axis=0, keepdims=True), axis=1, keepdims=True)


def pieces(value):
    first = value.astype(BF16).astype(F32)
    rest = value - first
    second = rest.astype(BF16).astype(F32)
    return first, second, (rest - second)


def wrap(target, count):
    for _ in range(3):
        target = jnp.where(target >= count, target - count, target)
    return target


class Shape:
    def __init__(self, tiles, cap, width, nl, nr, noff):
        self.tiles, self.cap, self.width, self.nl, self.nr, self.noff = tiles, cap, width, nl, nr, noff
        self.send_cap = max(2, 2 * cap * nr // tiles)
        self.slots = max(16, self.send_cap)
        self.fold = 2 if self.slots % 32 == 0 else 1
        self.full = width // LANES
        self.rest = width - self.full * LANES
        self.tail = self.slots // self.fold
        self.head = self.full * self.slots
        self.extra = self.head + self.tail
        self.rows = self.extra + 16
        self.per = LANES // self.slots
        self.chunks = tiles // self.per
        self.inbound = tiles * self.slots


def pack(sh, values, rank_ref, out_ref, sel_ref):
    for d in range(sh.tiles):
        picked = (rank_ref[d : d + 1, :] == iota((sh.slots, sh.cap), 0)).astype(F32).astype(BF16)
        sel_ref[d * sh.slots : (d + 1) * sh.slots, :] = picked
    rows = dot(sel_ref[...], values).astype(BF16)
    for d in range(sh.tiles):
        block = rows[d * sh.slots : (d + 1) * sh.slots]
        for p in range(sh.full):
            out_ref[d, p * sh.slots : (p + 1) * sh.slots, :] = block[:, p * LANES : (p + 1) * LANES]
        last = block[:, sh.full * LANES :]
        if sh.fold == 2:
            last = jnp.concatenate([last[: sh.tail], last[sh.tail :]], axis=1)
        else:
            last = jnp.concatenate([last, jnp.zeros_like(last)], axis=1)
        out_ref[d, sh.head : sh.extra, :] = last


def sum_rows(sums):
    row = iota((16, LANES), 0)
    tile = jnp.zeros((16, LANES), F32)
    for q, value in enumerate(sums):
        for p, piece in enumerate(pieces(value)):
            tile = jnp.where(row == 4 + 3 * q + p, piece, tile)
    return tile


def first_kernel(sh, mine_ref, counts_ref, rhs_ref, tile_ref, target_ref, offset_ref,
                 start_ref, rank_out, out_ref, sel_ref, rank_ref):
    mine = mine_ref[0]
    count = counts_ref[mine]
    live = (iota((sh.cap, 1), 0) < count).astype(F32)
    start = rhs_ref[...] * live
    start_ref[...] = start
    tile = flip(tile_ref[...]).astype(jnp.int32)
    target = flip(target_ref[...])
    offset = flip(offset_ref[...])
    which = iota((sh.tiles, sh.cap), 0)
    named = jnp.zeros((sh.tiles, sh.cap), F32)
    targets = jnp.zeros((sh.tiles, sh.cap), F32)
    offsets = jnp.zeros((sh.tiles, sh.cap), F32)
    for r in range(sh.nr):
        hit = tile[r : r + 1, :] == which
        named = jnp.where(hit, 1.0, named)
        targets = jnp.where(hit, target[r : r + 1, :], targets)
        offsets = jnp.where(hit, offset[r : r + 1, :], offsets)
    before = (iota((sh.cap, sh.cap), 0) < iota((sh.cap, sh.cap), 1)).astype(F32).astype(BF16)
    rank = dot(named.astype(BF16), before).astype(jnp.int32)
    rank = jnp.where(named > 0.0, rank, -LANES)
    rank_ref[...] = rank
    rank_out[...] = rank
    pack(sh, start.astype(BF16), rank_ref, out_ref, sel_ref)
    sums = sum_rows([total(start * start)])
    shift = lax.rem(mine, sh.per) * sh.slots
    row = iota((16, LANES), 0)
    for d in range(sh.tiles):
        picked = (rank[d : d + 1, :] + shift == iota((LANES, sh.cap), 0)).astype(F32).astype(BF16)
        table = jnp.where(row == 0, targets[d : d + 1, :], 0.0)
        table = jnp.where(row == 1, offsets[d : d + 1, :], table)
        table = jnp.where(row == 2, named[d : d + 1, :], table)
        extra = dot_nt(table.astype(BF16), picked) + sums
        out_ref[d, sh.extra :, :] = extra.astype(BF16)


def local_kernel(sh, mine_ref, counts_ref, target_ref, offset_ref, pairs_ref, code_ref):
    count = counts_ref[mine_ref[0]]
    target = wrap(flip(target_ref[...]).astype(jnp.int32), count)
    code_ref[...] = target * sh.noff + flip(offset_ref[...]).astype(jnp.int32)

    def body(o, carry):
        mark = iota((sh.cap, sh.cap), 0) * sh.noff + o
        amount = jnp.zeros((sh.cap, sh.cap), F32)
        for n in range(sh.nl):
            amount = amount + (code_ref[n : n + 1, :] == mark).astype(F32)
        pairs_ref[o] = amount.astype(BF16)
        return carry

    lax.fori_loop(0, sh.noff, body, 0)


def next_vector(step, current, olds, sums):
    if step == 0:
        return current / jnp.sqrt(sums[0])
    square = sums[step]
    kept = current
    for j in range(step):
        square = square - sums[j] * sums[j]
        kept = kept - sums[j] * olds[j]
    return -kept / jnp.sqrt(square)


def step_kernel(sh, step, *refs):
    refs = list(refs)
    take = lambda n: [refs.pop(0) for _ in range(n)]
    mine_ref, counts_ref, recv_ref, rank_ref, pairs_ref, tmatrix_ref, lattice_ref, current_ref = take(8)
    olds = take(step)
    copies = take(step)
    code_in = take(1 if step else 0)
    vector_out, image_out, sums_out = take(3)
    last = step == ITERS - 1
    send_out = take(1)[0]
    copy_out = None if last else take(1)[0]
    code_out = take(0 if step else 1)
    lattice_vmem, sems, x_ref, p_ref, sel_ref = refs
    groups = sh.noff // GROUP
    loads = [
        pltpu.make_async_copy(
            lattice_ref.at[pl.ds(g * GROUP, GROUP)], lattice_vmem.at[pl.ds(g * GROUP, GROUP)], sems.at[g]
        )
        for g in range(groups)
    ]
    for load in loads:
        load.start()
    count = counts_ref[mine_ref[0]]
    extras = jnp.zeros((16, LANES), F32)
    for s in range(sh.tiles):
        extras = extras + recv_ref[s, sh.extra :, :].astype(F32)
    sums = []
    for q in range(max(1, step + 1)):
        r = 4 + 3 * q
        three = extras[r : r + 1, 0:1] + extras[r + 1 : r + 2, 0:1] + extras[r + 2 : r + 3, 0:1]
        sums.append(three)
    vector = next_vector(step, current_ref[...], [ref[...] for ref in olds], sums)
    vector_out[...] = vector
    x_ref[0 : sh.cap, :] = vector.astype(BF16)
    if step == 0:
        code_ref = code_out[0]
        for c in range(sh.chunks):
            table = jnp.zeros((16, LANES), F32)
            for s in range(c * sh.per, (c + 1) * sh.per):
                table = table + recv_ref[s, sh.extra :, :].astype(F32)
            target = wrap(table[0:1].astype(jnp.int32), count)
            code = target * sh.noff + table[1:2].astype(jnp.int32)
            code_ref[c : c + 1, :] = jnp.where(table[2:3] > 0.5, code, -1)
    else:
        code_ref = code_in[0]
    for s in range(sh.tiles):
        parts = [recv_ref[s, p * sh.slots : (p + 1) * sh.slots, :] for p in range(sh.full)]
        end = recv_ref[s, sh.head : sh.extra, :].astype(F32)
        if sh.fold == 2:
            end = jnp.concatenate([end[:, : sh.rest], end[:, sh.rest :]], axis=0)
        else:
            end = end[:, : sh.rest]
        block = jnp.concatenate([part.astype(F32) for part in parts] + [end], axis=1)
        a = s * sh.slots
        row = next_vector(step, block, [ref[a : a + sh.slots, :] for ref in copies], sums)
        if copy_out is not None:
            copy_out[a : a + sh.slots, :] = row
        x_ref[sh.cap + a : sh.cap + a + sh.slots, :] = row.astype(BF16)
    field = jnp.zeros((sh.cap, sh.width), F32)
    mark = iota((sh.cap, LANES), 0) * sh.noff
    for g in range(groups):
        for q in range(GROUP):
            o = g * GROUP + q
            p_ref[q * sh.cap : (q + 1) * sh.cap, 0 : sh.cap] = pairs_ref[o]
            for c in range(sh.chunks):
                hit = (code_ref[c : c + 1, :] - o == mark).astype(F32).astype(BF16)
                p_ref[q * sh.cap : (q + 1) * sh.cap, sh.cap + c * LANES : sh.cap + (c + 1) * LANES] = hit
        summed = dot(p_ref[...], x_ref[...]).astype(BF16)
        loads[g].wait()
        for q in range(GROUP):
            field = field + dot(summed[q * sh.cap : (q + 1) * sh.cap], lattice_vmem[g * GROUP + q])
    live = (iota((sh.cap, 1), 0) < count).astype(F32)
    image = live * dot(field.astype(BF16), tmatrix_ref[...])
    image_out[...] = image
    out = [total(ref[...] * image) for ref in olds] + [total(vector * image), total(image * image)]
    row8 = iota((8, LANES), 0)
    seen = jnp.zeros((8, LANES), F32)
    for q, value in enumerate(sums):
        seen = jnp.where(row8 == q, value, seen)
    sums_out[...] = seen
    if last:
        tile = jnp.zeros((8, LANES), F32)
        for q, value in enumerate(out):
            tile = jnp.where(row8 == q, value, tile)
        for d in range(sh.tiles):
            send_out[d] = tile
    else:
        pack(sh, image.astype(BF16), rank_ref, send_out, sel_ref)
        tile = sum_rows(out).astype(BF16)
        for d in range(sh.tiles):
            send_out[d, sh.extra :, :] = tile


def last_kernel(sh, recv_ref, *refs):
    seen = refs[:ITERS]
    vectors = refs[ITERS : 2 * ITERS]
    image_ref, basis_ref, hess_ref = refs[2 * ITERS :]
    final = jnp.zeros((8, LANES), F32)
    for s in range(sh.tiles):
        final = final + recv_ref[s]
    tables = [ref[...] for ref in seen[1:]] + [final]
    row = iota((ITERS + 1, ITERS), 0)
    col = iota((ITERS + 1, ITERS), 1)
    hess = jnp.zeros((ITERS + 1, ITERS), F32)
    for k in range(ITERS):
        square = tables[k][k + 1 : k + 2, 0:1]
        for j in range(k + 1):
            product = tables[k][j : j + 1, 0:1]
            square = square - product * product
            hess = jnp.where((row == j) & (col == k), (1.0 if j == k else 0.0) - product, hess)
        hess = jnp.where((row == k + 1) & (col == k), jnp.sqrt(square), hess)
    hess_ref[...] = hess
    sums = [final[q : q + 1, 0:1] for q in range(ITERS + 1)]
    olds = [ref[...] for ref in vectors]
    for j in range(ITERS):
        basis_ref[j] = olds[j]
    basis_ref[ITERS] = next_vector(ITERS, image_ref[...], olds, sums)


def call(kernel, name, outs, args, smem=0, hbm=(), scratch=()):
    whole = pl.BlockSpec(memory_space=pltpu.VMEM)
    specs = [
        pl.BlockSpec(memory_space=pltpu.SMEM if i < smem else pl.ANY) if i < smem or i in hbm else whole
        for i in range(len(args))
    ]
    return pl.pallas_call(
        kernel,
        name=name,
        out_shape=[jax.ShapeDtypeStruct(shape, dtype) for shape, dtype in outs],
        in_specs=specs,
        out_specs=[whole] * len(outs),
        scratch_shapes=list(scratch),
        compiler_params=pltpu.CompilerParams(vmem_limit_bytes=VMEM_LIMIT),
    )(*args)


def per_device(
    rhs,
    counts,
    local_target,
    local_offset,
    remote_tile,
    remote_target,
    remote_offset,
    lattice,
    tmatrix,
):
    tiles = lax.axis_size("tile")
    cap, width = rhs.shape
    noff = lattice.shape[0]
    sh = Shape(tiles, cap, width, local_target.shape[1], remote_tile.shape[1], noff)
    mine = lax.axis_index("tile").astype(jnp.int32).reshape(1)
    exchange = functools.partial(
        lax.all_to_all, axis_name="tile", split_axis=0, concat_axis=0, tiled=True
    )
    own = ((cap, width), F32)
    block = ((tiles, sh.rows, LANES), BF16)
    select = pltpu.VMEM((sh.inbound, cap), BF16)
    start, rank, send = call(
        functools.partial(first_kernel, sh),
        "first",
        [own, ((tiles, cap), jnp.int32), block],
        [mine, counts, rhs, remote_tile, remote_target, remote_offset],
        smem=2,
        scratch=[select, pltpu.VMEM((tiles, cap), jnp.int32)],
    )
    recv = exchange(send)
    (pairs,) = call(
        functools.partial(local_kernel, sh),
        "local_pairs",
        [((noff, cap, cap), BF16)],
        [mine, counts, local_target, local_offset],
        smem=2,
        scratch=[pltpu.VMEM((sh.nl, cap), jnp.int32)],
    )
    current, olds, copies, codes, seen = start, [], [], [], []
    for step in range(ITERS):
        last = step == ITERS - 1
        outs = [own, own, ((8, LANES), F32)]
        outs.append(((tiles, 8, LANES), F32) if last else block)
        if not last:
            outs.append(((sh.inbound, width), F32))
        if step == 0:
            outs.append(((sh.chunks, LANES), jnp.int32))
        result = call(
            functools.partial(step_kernel, sh, step),
            f"step{step}",
            outs,
            [mine, counts, recv, rank, pairs, tmatrix, lattice, current, *olds, *copies, *codes],
            smem=2,
            hbm=(6,),
            scratch=[
                pltpu.VMEM((noff, width, width), BF16),
                pltpu.SemaphoreType.DMA((noff // GROUP,)),
                pltpu.VMEM((cap + sh.inbound, width), BF16),
                pltpu.VMEM((GROUP * cap, cap + sh.inbound), BF16),
                select,
            ],
        )
        vector, current, sums, send = result[:4]
        olds.append(vector)
        seen.append(sums)
        if not last:
            copies.append(result[4])
        if step == 0:
            codes = [result[5]]
        recv = exchange(send)
    basis, hess = call(
        functools.partial(last_kernel, sh),
        "last",
        [((ITERS + 1, cap, width), F32), ((ITERS + 1, ITERS), F32)],
        [recv, *seen, *olds, current],
    )
    return basis, hess


def solution(mesh):
    placed = (
        P(("groups", "tile"), None),
        P("groups"),
        P(("groups", "tile"), None),
        P(("groups", "tile"), None),
        P(("groups", "tile"), None),
        P(("groups", "tile"), None),
        P(("groups", "tile"), None),
        P(),
        P(),
    )
    return jax.shard_map(
        per_device,
        mesh=mesh,
        in_specs=placed,
        out_specs=(P(None, ("groups", "tile"), None), P("groups", None)),
        check_vma=False,
    )
```

time: 593 us -> 141 us (0.24)
  blocking collectives: 338 us -> 58.8 us
  other arithmetic: 125 us -> 0 us
  Pallas kernels: 0 us -> 54.1 us
  local copies, waits for them, and re-layouts: 59.2 us -> 10.5 us
  waiting for transfers between devices: 29.2 us -> 8.81 us
  matrix products: 19.1 us -> 0 us
  starting transfers between devices: 14.6 us -> 7.36 us
  between operations: 6.84 us -> 0.7 us
    psum x10 -> x0, blocking collectives: 315 us -> none  [the longest x6 190 us: per_device(): product = lax.psum(jnp.sum(vectors[j] * image), 'tile')]
    scatter-add x3 -> x0, other arithmetic: 95.1 us -> none  [per_device(): summed = jax.ops.segment_sum(rows, codes, num_segments=dump + 1)]
    pallas_call x0 -> x6, Pallas kernels: none -> 54.1 us  [call(): pl.pallas_call(kernel, name=name, out_shape=[jax.ShapeDtypeStruct(shape,...]
    all_to_all x1 -> x3, blocking collectives: 22.8 us -> 58.8 us  [per_device(): recv = exchange(send)]
    all_to_all x3 -> x1, waiting for transfers between devices: 29.2 us -> 8.81 us  [per_device(): recv = exchange(send)]
    dot_general x3 -> x0, matrix products: 19.1 us -> none  [per_device(): scattered = jnp.dot(field, tmatrix, preferred_element_type=jnp.float32)]
    gather x4 -> x0, local copies, waits for them, and re-layouts: 15.8 us -> none  [the longest x3 13.8 us: per_device(): rows_out = padded[inverse].reshape(tiles, send_cap, width)]
    convert_element_type x6 -> x0, local copies, waits for them, and re-layouts: 13 us -> none  [the longest x3 12.6 us: per_device(): summed = summed[:dump].reshape(cap, noff * width).astype(jnp.bfloat16)]
  transfers between devices with their start and end apart: 3 -> 1, of which waited for: 2 -> 1; matrix products, arithmetic and copies ran while one was open for 3% -> 1% of each run, Pallas kernels for 0% -> 5%
where the time goes in v1:
time: 141 us; the launch traced here: 140 us
  blocking collectives  58.8 us (42%)
  Pallas kernels  54.1 us (38%)
  local copies, waits for them, and re-layouts  10.5 us (7%)
  waiting for transfers between devices  8.81 us (6%)
  starting transfers between devices  7.36 us (5%)
    all_to_all x3, blocking collectives, per_device(): recv = exchange(send)  58.8 us
    pallas_call x6, Pallas kernels, call(): pl.pallas_call(kernel, name=name, out_shape=[jax.ShapeDtypeStruct(shape,...  54.1 us
    all_to_all x1, waiting for transfers between devices, per_device(): recv = exchange(send)  8.81 us
    unnamed x12, local copies, waits for them, and re-layouts  8.29 us
    all_to_all x1, starting transfers between devices, per_device(): recv = exchange(send)  7.36 us
  transfers between devices with their start and end apart: 1, of which 1 were waited for; matrix products, arithmetic and copies ran while one was open for 1% of the time, Pallas kernels for 5%

profile of v1, /device:TPU:0, one launch (start us, length us, event | category | flops | bytes accessed | tf_op | source)
XLA Modules:
  0.0 140.2 jit_solution(17516855807147341172)
XLA Ops:
  0.6 0.0 copy-start.1
  0.6 0.0 copy-start.2
  0.7 1.4 %copy.12.tile_ref = s32[128,4]{1,0:T(8,128)} copy(s32[128,4]{0,1:T(4,128)} %param.13) | data formatting | bytes 4096 | tf_op args[4]
  2.1 1.4 %copy.13.target_ref = s32[128,4]{1,0:T(8,128)} copy(s32[128,4]{0,1:T(4,128)} %param.14) | data formatting | bytes 4096 | tf_op args[5]
  3.5 1.4 copy.14.offset_ref
  4.9 1.7 %copy.11.rhs_ref = f32[128,320]{1,0:T(8,128)} copy(f32[128,320]{0,1:T(8,128)} %param.9) | data formatting | bytes 327680 | tf_op args[0]
  6.6 2.8 %first.1 = (f32[128,320]{1,0:T(8,128)}, s32[16,128]{1,0:T(8,128)}, bf16[16,176,128]{2,1,0:T(8,128)(2,1)}) custom-call(s32[1]{0:T(128)} %bitcast.mine_ref.refs_0_, s32[16]{0:T(128)} %refs_1_.5, f32[128,320]{1,0:T(8,128)} %copy.11.rhs_ref, s32[128,4]{1,0:T(8,128)} %copy.12.tile_ref, s32[128,4]{1,0:T(8,128)} %copy.13.target_ref, s32[128,4]{1,0:T(8,128)} %copy.14.offset_ref), custom_call_target="tpu_custom_call" | custom-call | tf_op jit(solution)/shard_map/first/pallas_call | solution.py:287
  9.4 7.4 %all-to-all-start = ((bf16[16,176,128]{2,1,0:T(8,128)(2,1)}), bf16[16,176,128]{2,1,0:T(8,128)(2,1)S(1)}, u32[]{:S(2)}, u32[]{:S(2)}) async-start(bf16[16,176,128]{2,1,0:T(8,128)(2,1)} %get-tuple-element.20), calls=%async_computation | async-start | bytes 1441792 | tf_op jit(solution)/shard_map/all_to_all | solution.py:328
  16.8 0.0 copy-done.1
  16.8 0.7 copy.15.target_ref
  17.5 0.0 copy-done.2
  17.5 0.7 copy.16.offset_ref
  18.2 7.4 %local_pairs.1.refs_4_ = bf16[32,128,128]{2,1,0:T(8,128)(2,1)} custom-call(s32[1]{0:T(128)} %bitcast.mine_ref.refs_0_, s32[16]{0:T(128)} %refs_1_.5, s32[128,24]{1,0:T(8,128)} %copy.15.target_ref, s32[128,24]{1,0:T(8,128)} %copy.16.offset_ref), custom_call_target="tpu_custom_call" | custom-call | tf_op jit(solution)/shard_map/local_pairs/pallas_call | solution.py:287
  25.6 8.8 %all-to-all-done.refs_2_ = bf16[16,176,128]{2,1,0:T(8,128)(2,1)S(1)} async-done(((bf16[16,176,128]{2,1,0:T(8,128)(2,1)}), bf16[16,176,128]{2,1,0:T(8,128)(2,1)S(1)}, u32[]{:S(2)}, u32[]{:S(2)}) %all-to-all-start) | async-done | bytes 720928 | tf_op jit(solution)/shard_map/all_to_all | solution.py:328
  34.4 0.0 copy-start
  34.4 0.9 copy-done
  35.3 13.5 %step0.1 = (f32[128,320]{1,0:T(8,128)}, f32[128,320]{1,0:T(8,128)}, f32[8,128]{1,0:T(8,128)}, bf16[16,176,128]{2,1,0:T(8,128)(2,1)}, f32[1024,320]{1,0:T(8,128)}, /*index=5*/s32[8,128]{1,0:T(8,128)}) custom-call(s32[1]{0:T(128)} %bitcast.mine_ref.refs_0_, s32[16]{0:T(128)} %refs_1_.5, bf16[16,176,128]{2,1,0:T(8,128)(2,1)} %copy-done, ...), custom_call_target="tpu_custom_call" | custom-call | tf_op jit(solution)/shard_map/step0/pallas_call | solution.py:287
  48.8 24.4 %all_to_all.20.refs_2_ = bf16[16,176,128]{2,1,0:T(8,128)(2,1)} all-to-all(bf16[16,176,128]{2,1,0:T(8,128)(2,1)} %get-tuple-element.23), channel_id=1, replica_groups=mesh['groups'=2,'tile'=16] {'tile'}, dimensions={0} | all-to-all | bytes 1441792 | tf_op jit(solution)/shard_map/all_to_all | solution.py:368
  73.2 14.2 %step1.1 = (f32[128,320]{1,0:T(8,128)}, f32[128,320]{1,0:T(8,128)}, f32[8,128]{1,0:T(8,128)}, bf16[16,176,128]{2,1,0:T(8,128)(2,1)}, f32[1024,320]{1,0:T(8,128)}) custom-call(s32[1]{0:T(128)} %bitcast.mine_ref.refs_0_, s32[16]{0:T(128)} %refs_1_.5, bf16[16,176,128]{2,1,0:T(8,128)(2,1)} %all_to_all.20.refs_2_, s32[16,128]{1,0:T(8,128)} %get-tuple-element.21.refs_3_, ...), custom_call_target="tpu_custom_call" | custom-call | tf_op jit(solution)/shard_map/step1/pallas_call | solution.py:287
  87.3 23.4 %all_to_all.21.refs_2_ = bf16[16,176,128]{2,1,0:T(8,128)(2,1)} all-to-all(bf16[16,176,128]{2,1,0:T(8,128)(2,1)} %get-tuple-element.28), channel_id=1, replica_groups=mesh['groups'=2,'tile'=16] {'tile'}, dimensions={0} | all-to-all | bytes 1441792 | tf_op jit(solution)/shard_map/all_to_all | solution.py:368
  110.7 13.9 %step2.1 = (f32[128,320]{1,0:T(8,128)}, f32[128,320]{1,0:T(8,128)}, f32[8,128]{1,0:T(8,128)}, f32[16,8,128]{2,1,0:T(8,128)}) custom-call(s32[1]{0:T(128)} %bitcast.mine_ref.refs_0_, s32[16]{0:T(128)} %refs_1_.5, bf16[16,176,128]{2,1,0:T(8,128)(2,1)} %all_to_all.21.refs_2_, s32[16,128]{1,0:T(8,128)} %get-tuple-element.21.refs_3_, ...), custom_call_target="tpu_custom_call" | custom-call | tf_op jit(solution)/shard_map/step2/pallas_call | solution.py:287
  124.6 11.0 %all_to_all.22.recv_ref = f32[16,8,128]{2,1,0:T(8,128)} all-to-all(f32[16,8,128]{2,1,0:T(8,128)} %get-tuple-element.32), channel_id=1, replica_groups=mesh['groups'=2,'tile'=16] {'tile'}, dimensions={0} | all-to-all | bytes 131072 | tf_op jit(solution)/shard_map/all_to_all | solution.py:368
  135.7 2.4 %last.1 = (f32[4,128,320]{2,1,0:T(8,128)}, f32[4,3]{1,0:T(4,128)}) custom-call(f32[16,8,128]{2,1,0:T(8,128)} %all_to_all.22.recv_ref, f32[8,128]{1,0:T(8,128)} %get-tuple-element.33.refs_0_, f32[8,128]{1,0:T(8,128)} %get-tuple-element.34.refs_1_, f32[8,128]{1,0:T(8,128)} %get-tuple-element.35.refs_2_, f32[128,320]{1,0:T(8,128)} %get-tuple-element.25.refs_8_.refs_3_, ...), custom_call_target="tpu_custom_call" | custom-call | tf_op jit(solution)/shard_map/last/pallas_call | solution.py:287
  138.0 2.2 %copy.17 = f32[4,128,320]{1,2,0:T(8,128)} copy(f32[4,128,320]{2,1,0:T(8,128)} %get-tuple-element.38) | data formatting | bytes 1310720 | tf_op jit(solution)/shard_map/last/pallas_call | solution.py:287
Async XLA Ops:
  0.6 16.1 %copy-start.1 = (s32[128,24]{0,1:T(8,128)S(1)}, s32[128,24]{0,1:T(8,128)}, u32[]{:S(2)}) copy-start(s32[128,24]{0,1:T(8,128)} %param.11) | copy-start | bytes 36868
  0.6 16.9 %copy-start.2 = (s32[128,24]{0,1:T(8,128)S(1)}, s32[128,24]{0,1:T(8,128)}, u32[]{:S(2)}) copy-start(s32[128,24]{0,1:T(8,128)} %param.12) | copy-start | bytes 36868
  9.4 25.0 %all-to-all-start = ((bf16[16,176,128]{2,1,0:T(8,128)(2,1)}), bf16[16,176,128]{2,1,0:T(8,128)(2,1)S(1)}, u32[]{:S(2)}, u32[]{:S(2)}) async-start(bf16[16,176,128]{2,1,0:T(8,128)(2,1)} %get-tuple-element.20), calls=%async_computation | async-start | bytes 1441792 | tf_op jit(solution)/shard_map/all_to_all | solution.py:328
  34.4 0.9 copy-start

commit v2 on v1

v2 whole, which is shorter than its diff:
```python
import functools

import jax
import jax.numpy as jnp
from jax import lax
from jax.experimental import pallas as pl
from jax.experimental.pallas import tpu as pltpu
from jax.sharding import PartitionSpec as P

ITERS = 3
LANES = 128
GROUP = 4
F32 = jnp.float32
BF16 = jnp.bfloat16
VMEM_LIMIT = 56 * 1024 * 1024


def iota(shape, dim):
    return lax.broadcasted_iota(jnp.int32, shape, dim)


def dot(a, b):
    return lax.dot_general(a, b, (((1,), (0,)), ((), ())), preferred_element_type=F32)


def dot_nt(a, b):
    return lax.dot_general(a, b, (((1,), (1,)), ((), ())), preferred_element_type=F32)


def dot_tn(a, b):
    return lax.dot_general(a, b, (((0,), (0,)), ((), ())), preferred_element_type=F32)


def flag(mask):
    return mask.astype(F32).astype(BF16)


def identity(size):
    return flag(iota((size, size), 0) == iota((size, size), 1))


def total(values):
    return jnp.sum(jnp.sum(values, axis=0, keepdims=True), axis=1, keepdims=True)


def pieces(value):
    first = value.astype(BF16).astype(F32)
    rest = value - first
    second = rest.astype(BF16).astype(F32)
    return first, second, rest - second


def wrap(target, count):
    for _ in range(3):
        target = jnp.where(target >= count, target - count, target)
    return target


def each(amount, body):
    if amount <= 16:
        for i in range(amount):
            body(i)
    else:
        lax.fori_loop(0, amount, lambda i, carry: (body(i), carry)[1], 0)


class Shape:
    def __init__(self, tiles, cap, width, nl, nr, noff):
        self.tiles, self.cap, self.width, self.nl, self.nr, self.noff = tiles, cap, width, nl, nr, noff
        self.send_cap = max(2, 2 * cap * nr // tiles)
        self.slots = max(16, self.send_cap)
        self.fold = LANES // self.slots
        self.part = width // self.fold
        self.extra = -(-self.part // 16) * 16
        self.rows = self.extra + 16
        self.chunks = tiles // self.fold
        self.inbound = self.chunks * LANES
        self.sources = cap + self.inbound


def pack(sh, mine, values, rank_ref, out_ref):
    parts = [values[f * sh.part : (f + 1) * sh.part] for f in range(sh.fold)]
    wide = jnp.concatenate(parts, axis=1)
    lane = iota((LANES, sh.cap), 0)
    shifts = [lax.rem(mine + f, sh.fold) * sh.slots for f in range(sh.fold)]

    def body(d):
        rank = rank_ref[pl.ds(d, 1), :]
        picked = jnp.concatenate([flag(rank + shift == lane) for shift in shifts], axis=1)
        block = dot_nt(wide, picked).astype(BF16)
        if sh.extra > sh.part:
            block = jnp.concatenate([block, jnp.zeros((sh.extra - sh.part, LANES), BF16)], axis=0)
        out_ref[d, 0 : sh.extra, :] = block

    each(sh.tiles, body)


def sum_rows(sums):
    row = iota((16, LANES), 0)
    tile = jnp.zeros((16, LANES), F32)
    for q, value in enumerate(sums):
        for p, piece in enumerate(pieces(value)):
            tile = jnp.where(row == 4 + 3 * q + p, piece, tile)
    return tile


def first_kernel(sh, mine_ref, counts_ref, rhs_ref, tile_ref, target_ref, offset_ref,
                 start_ref, rank_ref, out_ref, code_ref):
    mine = mine_ref[0]
    count = counts_ref[mine]
    start = rhs_ref[...] * (iota((1, sh.cap), 1) < count).astype(F32)
    start_ref[...] = start
    tile = tile_ref[...]
    target = target_ref[...].astype(F32)
    offset = offset_ref[...].astype(F32)
    which = iota((sh.tiles, sh.cap), 0)
    named = jnp.zeros((sh.tiles, sh.cap), F32)
    targets = jnp.zeros((sh.tiles, sh.cap), F32)
    offsets = jnp.zeros((sh.tiles, sh.cap), F32)
    for r in range(sh.nr):
        hit = tile[r : r + 1, :] == which
        named = jnp.where(hit, 1.0, named)
        targets = jnp.where(hit, target[r : r + 1, :], targets)
        offsets = jnp.where(hit, offset[r : r + 1, :], offsets)
    before = flag(iota((sh.cap, sh.cap), 0) < iota((sh.cap, sh.cap), 1))
    rank = dot(named.astype(BF16), before).astype(jnp.int32)
    rank_ref[...] = jnp.where(named > 0.0, rank, -2 * LANES)
    code_ref[0] = targets
    code_ref[1] = offsets
    code_ref[2] = named
    pack(sh, mine, start.astype(BF16), rank_ref, out_ref)
    sums = sum_rows([total(start * start)])
    shift = lax.rem(mine, sh.fold) * sh.slots
    row = iota((16, LANES), 0)
    lane = iota((LANES, sh.cap), 0)

    def body(d):
        picked = flag(rank_ref[pl.ds(d, 1), :] + shift == lane)
        table = jnp.zeros((16, sh.cap), F32)
        for q in range(3):
            table = jnp.where(row == q, code_ref[q, pl.ds(d, 1), :], table)
        extra = dot_nt(table.astype(BF16), picked) + sums
        out_ref[d, sh.extra :, :] = extra.astype(BF16)

    each(sh.tiles, body)


def tables_kernel(sh, mine_ref, counts_ref, target_ref, offset_ref, tmatrix_ref, lattice_ref,
                  pairs_ref, flipped_ref, turned_ref, code_ref, lattice_vmem, sems):
    groups = sh.noff // GROUP
    loads = [
        pltpu.make_async_copy(
            lattice_ref.at[pl.ds(g * GROUP, GROUP)], lattice_vmem.at[pl.ds(g * GROUP, GROUP)], sems.at[g]
        )
        for g in range(groups)
    ]
    for load in loads:
        load.start()
    count = counts_ref[mine_ref[0]]
    code_ref[...] = wrap(target_ref[...], count) * sh.noff + offset_ref[...]
    eye = identity(sh.cap)

    def body(o, carry):
        mark = iota((sh.cap, sh.cap), 0) * sh.noff + o
        amount = jnp.zeros((sh.cap, sh.cap), F32)
        for n in range(sh.nl):
            amount = amount + (code_ref[n : n + 1, :] == mark).astype(F32)
        pairs_ref[o] = dot_nt(eye, amount.astype(BF16)).astype(BF16)
        return carry

    lax.fori_loop(0, sh.noff, body, 0)
    wide = identity(sh.width)
    turned_ref[...] = dot_nt(wide, tmatrix_ref[...]).astype(BF16)
    for g in range(groups):
        loads[g].wait()
        some = lattice_vmem[g * GROUP : (g + 1) * GROUP].reshape(GROUP * sh.width, sh.width)
        span = GROUP * sh.width
        flipped_ref[:, g * span : (g + 1) * span] = dot_nt(wide, some).astype(BF16)


def next_vector(step, current, olds, sums):
    if step == 0:
        return current / jnp.sqrt(sums[0])
    square = sums[step]
    kept = current
    for j in range(step):
        square = square - sums[j] * sums[j]
        kept = kept - sums[j] * olds[j]
    return -kept / jnp.sqrt(square)


def step_kernel(sh, step, *refs):
    refs = list(refs)
    take = lambda n: [refs.pop(0) for _ in range(n)]
    mine_ref, counts_ref, recv_ref, rank_ref, pairs_ref, turned_ref, flipped_ref, current_ref = take(8)
    olds = take(step)
    copies = take(step)
    key_in = take(1 if step else 0)
    vector_out, image_out, sums_out, send_out = take(4)
    last = step == ITERS - 1
    copy_out = None if last else take(1)[0]
    key_out = take(0 if step else 1)
    flipped_vmem, sems, x_ref, p_ref = refs
    groups = sh.noff // GROUP
    span = GROUP * sh.width
    loads = [
        pltpu.make_async_copy(
            flipped_ref.at[:, pl.ds(g * span, span)], flipped_vmem.at[:, pl.ds(g * span, span)], sems.at[g]
        )
        for g in range(groups)
    ]
    for load in loads:
        load.start()
    mine = mine_ref[0]
    count = counts_ref[mine]
    extras = jnp.zeros((16, LANES), F32)
    for s in range(sh.tiles):
        extras = extras + recv_ref[s, sh.extra :, :].astype(F32)
    sums = []
    for q in range(max(1, step + 1)):
        r = 4 + 3 * q
        sums.append(extras[r : r + 1, 0:1] + extras[r + 1 : r + 2, 0:1] + extras[r + 2 : r + 3, 0:1])
    vector = next_vector(step, current_ref[...], [ref[...] for ref in olds], sums)
    vector_out[...] = vector
    x_ref[:, 0 : sh.cap] = vector.astype(BF16)
    if step == 0:
        key_ref = key_out[0]
        row = iota((16, LANES), 0)
        weight = jnp.where(row == 0, sh.noff, 0) + jnp.where(row == 1, 1, 0)
        weight = weight - jnp.where(row == 2, iota((16, LANES), 1) * sh.noff, 0)
        weight = (weight - jnp.where(row == 3, 16384, 0)).astype(F32).astype(BF16)
        for c in range(sh.chunks):
            table = jnp.zeros((16, LANES), F32)
            for s in range(c * sh.fold, (c + 1) * sh.fold):
                table = table + recv_ref[s, sh.extra :, :].astype(F32)
            target = wrap(table[0:1].astype(jnp.int32), count).astype(F32)
            empty = 1.0 - table[2:3]
            table = jnp.where(row == 0, target, table)
            table = jnp.where(row == 3, empty, jnp.where(row > 3, 0.0, table))
            key_ref[c * LANES : (c + 1) * LANES, :] = dot_tn(table.astype(BF16), weight)
    else:
        key_ref = key_in[0]
    lane_group = iota((1, LANES), 1) // sh.slots
    for c in range(sh.chunks):
        parts = []
        for f in range(sh.fold):
            part = recv_ref[c * sh.fold, 0 : sh.extra, :].astype(F32)[: sh.part]
            for m in range(1, sh.fold):
                other = recv_ref[c * sh.fold + m, 0 : sh.extra, :].astype(F32)[: sh.part]
                part = jnp.where(lane_group == (m + f) % sh.fold, other, part)
            if f:
                part = pltpu.roll(part, LANES - f * sh.slots, 1)
            parts.append(part)
        a = c * LANES
        column = next_vector(
            step, jnp.concatenate(parts, axis=0), [ref[:, a : a + LANES] for ref in copies], sums
        )
        if copy_out is not None:
            copy_out[:, a : a + LANES] = column
        x_ref[:, sh.cap + a : sh.cap + a + LANES] = column.astype(BF16)
    field = jnp.zeros((sh.width, sh.cap), F32)
    for g in range(groups):
        for q in range(GROUP):
            o = g * GROUP + q
            cols = slice(q * sh.cap, (q + 1) * sh.cap)
            p_ref[0 : sh.cap, cols] = pairs_ref[o]
            for c in range(sh.chunks):
                a = c * LANES
                p_ref[sh.cap + a : sh.cap + a + LANES, cols] = flag(key_ref[a : a + LANES, :] == float(o))
        summed = dot(x_ref[...], p_ref[...]).astype(BF16)
        stack = jnp.concatenate([summed[:, q * sh.cap : (q + 1) * sh.cap] for q in range(GROUP)], axis=0)
        loads[g].wait()
        field = field + dot(flipped_vmem[:, g * span : (g + 1) * span], stack)
    live = (iota((1, sh.cap), 1) < count).astype(F32)
    image = live * dot(turned_ref[...], field.astype(BF16))
    image_out[...] = image
    out = [total(ref[...] * image) for ref in olds] + [total(vector * image), total(image * image)]
    row8 = iota((8, LANES), 0)
    seen = jnp.zeros((8, LANES), F32)
    for q, value in enumerate(sums):
        seen = jnp.where(row8 == q, value, seen)
    sums_out[...] = seen
    if last:
        tile = jnp.zeros((8, LANES), F32)
        for q, value in enumerate(out):
            tile = jnp.where(row8 == q, value, tile)
        for d in range(sh.tiles):
            send_out[d] = tile
    else:
        pack(sh, mine, image.astype(BF16), rank_ref, send_out)
        tile = sum_rows(out).astype(BF16)
        for d in range(sh.tiles):
            send_out[d, sh.extra :, :] = tile


def last_kernel(sh, recv_ref, *refs):
    seen = refs[:ITERS]
    vectors = refs[ITERS : 2 * ITERS]
    image_ref, basis_ref, hess_ref = refs[2 * ITERS :]
    final = jnp.zeros((8, LANES), F32)
    for s in range(sh.tiles):
        final = final + recv_ref[s]
    tables = [ref[...] for ref in seen[1:]] + [final]
    row = iota((ITERS + 1, ITERS), 0)
    col = iota((ITERS + 1, ITERS), 1)
    hess = jnp.zeros((ITERS + 1, ITERS), F32)
    for k in range(ITERS):
        square = tables[k][k + 1 : k + 2, 0:1]
        for j in range(k + 1):
            product = tables[k][j : j + 1, 0:1]
            square = square - product * product
            hess = jnp.where((row == j) & (col == k), (1.0 if j == k else 0.0) - product, hess)
        hess = jnp.where((row == k + 1) & (col == k), jnp.sqrt(square), hess)
    hess_ref[...] = hess
    sums = [final[q : q + 1, 0:1] for q in range(ITERS + 1)]
    olds = [ref[...] for ref in vectors]
    for j in range(ITERS):
        basis_ref[j] = olds[j]
    basis_ref[ITERS] = next_vector(ITERS, image_ref[...], olds, sums)


def call(kernel, name, outs, args, smem=0, hbm=(), scratch=()):
    whole = pl.BlockSpec(memory_space=pltpu.VMEM)
    specs = [
        pl.BlockSpec(memory_space=pltpu.SMEM if i < smem else pl.ANY) if i < smem or i in hbm else whole
        for i in range(len(args))
    ]
    return pl.pallas_call(
        kernel,
        name=name,
        out_shape=[jax.ShapeDtypeStruct(shape, dtype) for shape, dtype in outs],
        in_specs=specs,
        out_specs=[whole] * len(outs),
        scratch_shapes=list(scratch),
        compiler_params=pltpu.CompilerParams(vmem_limit_bytes=VMEM_LIMIT),
    )(*args)


def per_device(
    rhs,
    counts,
    local_target,
    local_offset,
    remote_tile,
    remote_target,
    remote_offset,
    lattice,
    tmatrix,
):
    tiles = lax.axis_size("tile")
    cap, width = rhs.shape
    noff = lattice.shape[0]
    groups = noff // GROUP
    sh = Shape(tiles, cap, width, local_target.shape[1], remote_tile.shape[1], noff)
    mine = lax.axis_index("tile").astype(jnp.int32).reshape(1)
    exchange = functools.partial(
        lax.all_to_all, axis_name="tile", split_axis=0, concat_axis=0, tiled=True
    )
    own = ((width, cap), F32)
    block = ((tiles, sh.rows, LANES), BF16)
    start, rank, send = call(
        functools.partial(first_kernel, sh),
        "first",
        [own, ((tiles, cap), jnp.int32), block],
        [mine, counts, rhs.T, remote_tile.T, remote_target.T, remote_offset.T],
        smem=2,
        scratch=[pltpu.VMEM((3, tiles, cap), F32)],
    )
    recv = exchange(send)
    pairs, flipped, turned = call(
        functools.partial(tables_kernel, sh),
        "tables",
        [((noff, cap, cap), BF16), ((width, noff * width), BF16), ((width, width), BF16)],
        [mine, counts, local_target.T, local_offset.T, tmatrix, lattice],
        smem=2,
        hbm=(5,),
        scratch=[
            pltpu.VMEM((sh.nl, cap), jnp.int32),
            pltpu.VMEM((noff, width, width), BF16),
            pltpu.SemaphoreType.DMA((groups,)),
        ],
    )
    current, olds, copies, keys, seen = start, [], [], [], []
    for step in range(ITERS):
        last = step == ITERS - 1
        outs = [own, own, ((8, LANES), F32)]
        outs.append(((tiles, 8, LANES), F32) if last else block)
        if not last:
            outs.append(((width, sh.inbound), F32))
        if step == 0:
            outs.append(((sh.inbound, LANES), F32))
        result = call(
            functools.partial(step_kernel, sh, step),
            f"step{step}",
            outs,
            [mine, counts, recv, rank, pairs, turned, flipped, current, *olds, *copies, *keys],
            smem=2,
            hbm=(6,),
            scratch=[
                pltpu.VMEM((width, noff * width), BF16),
                pltpu.SemaphoreType.DMA((groups,)),
                pltpu.VMEM((width, sh.sources), BF16),
                pltpu.VMEM((sh.sources, GROUP * cap), BF16),
            ],
        )
        vector, current, sums, send = result[:4]
        olds.append(vector)
        seen.append(sums)
        if not last:
            copies.append(result[4])
        if step == 0:
            keys = [result[5]]
        recv = exchange(send)
    basis, hess = call(
        functools.partial(last_kernel, sh),
        "last",
        [((ITERS + 1, width, cap), F32), ((ITERS + 1, ITERS), F32)],
        [recv, *seen, *olds, current],
    )
    return jnp.transpose(basis, (0, 2, 1)), hess


def solution(mesh):
    placed = (
        P(("groups", "tile"), None),
        P("groups"),
        P(("groups", "tile"), None),
        P(("groups", "tile"), None),
        P(("groups", "tile"), None),
        P(("groups", "tile"), None),
        P(("groups", "tile"), None),
        P(),
        P(),
    )
    return jax.shard_map(
        per_device,
        mesh=mesh,
        in_specs=placed,
        out_specs=(P(None, ("groups", "tile"), None), P("groups", None)),
        check_vma=False,
    )
```

time: 141 us -> 133 us (0.943)
  local copies, waits for them, and re-layouts: 10.5 us -> 0.87 us
  Pallas kernels: 54.1 us -> 63.3 us
  waiting for transfers between devices: 8.81 us -> 0.01 us
    pallas_call x6, Pallas kernels: 54.1 us -> 63.3 us  [call(): pl.pallas_call(kernel, name=name, out_shape=[jax.ShapeDtypeStruct(shape,...]
    all_to_all x1, waiting for transfers between devices: 8.81 us -> 0.01 us  [per_device(): recv = exchange(send)]
    unnamed x12 -> x2, local copies, waits for them, and re-layouts: 8.29 us -> 0.87 us
    pallas_call x1 -> x0, local copies, waits for them, and re-layouts: 2.24 us -> none  [call(): pl.pallas_call(kernel, name=name, out_shape=[jax.ShapeDtypeStruct(shape,...]
  transfers between devices with their start and end apart: 1 -> 1, of which waited for: 1 -> 0; matrix products, arithmetic and copies ran while one was open for 1% -> 0% of each run, Pallas kernels for 5% -> 15%
where the time goes in v2:
time: 133 us; the launch traced here: 132 us
  Pallas kernels  63.3 us (48%)
  blocking collectives  59.7 us (45%)
  starting transfers between devices  7.36 us (6%)
    pallas_call x6, Pallas kernels, call(): pl.pallas_call(kernel, name=name, out_shape=[jax.ShapeDtypeStruct(shape,...  63.3 us
    all_to_all x3, blocking collectives, per_device(): recv = exchange(send)  59.7 us
    all_to_all x1, starting transfers between devices, per_device(): recv = exchange(send)  7.36 us
  transfers between devices with their start and end apart: 1, of which 0 were waited for; matrix products, arithmetic and copies ran while one was open for 0% of the time, Pallas kernels for 15%

profile of v2, /device:TPU:0, one launch (start us, length us, event | category | flops | bytes accessed | tf_op | source)
XLA Modules:
  0.0 131.9 jit_solution(8471633393974339368)
XLA Ops:
  0.6 2.7 %first.1 = (f32[320,128]{1,0:T(8,128)}, s32[16,128]{1,0:T(8,128)}, bf16[16,176,128]{2,1,0:T(8,128)(2,1)}) custom-call(s32[1]{0:T(128)} %bitcast.mine_ref.refs_0_, s32[16]{0:T(128)} %refs_1_.5, f32[320,128]{1,0:T(8,128)} %bitcast.8, s32[4,128]{1,0:T(4,128)} %bitcast.11, s32[4,128]{1,0:T(4,128)} %bitcast.12, s32[4,128]{1,0:T(4,128)} %bitcast.13), custom_call_target="tpu_custom_call" | custom-call | tf_op jit(solution)/shard_map/first/pallas_call | solution.py:328
  3.4 7.4 %all-to-all-start = ((bf16[16,176,128]{2,1,0:T(8,128)(2,1)}), bf16[16,176,128]{2,1,0:T(8,128)(2,1)S(1)}, u32[]{:S(2)}, u32[]{:S(2)}) async-start(bf16[16,176,128]{2,1,0:T(8,128)(2,1)} %get-tuple-element.25), calls=%async_computation | async-start | bytes 1441792 | tf_op jit(solution)/shard_map/all_to_all | solution.py:369
  10.7 19.3 %tables.1 = (bf16[32,128,128]{2,1,0:T(8,128)(2,1)}, bf16[320,10240]{1,0:T(8,128)(2,1)}, bf16[320,320]{1,0:T(8,128)(2,1)}) custom-call(s32[1]{0:T(128)} %bitcast.mine_ref.refs_0_, s32[16]{0:T(128)} %refs_1_.5, s32[24,128]{1,0:T(8,128)} %bitcast.9, s32[24,128]{1,0:T(8,128)} %bitcast.10, bf16[320,320]{1,0:T(8,128)(2,1)} %tmatrix_ref.1, ...), custom_call_target="tpu_custom_call" | custom-call | tf_op jit(solution)/shard_map/tables/pallas_call | solution.py:328
  30.0 0.0 all-to-all-done.refs_2_
  30.0 0.0 copy-start
  30.0 0.9 copy-done
  30.9 12.8 %step0.1 = (f32[320,128]{1,0:T(8,128)}, f32[320,128]{1,0:T(8,128)}, f32[8,128]{1,0:T(8,128)}, bf16[16,176,128]{2,1,0:T(8,128)(2,1)}, f32[320,1024]{1,0:T(8,128)}, /*index=5*/f32[1024,128]{1,0:T(8,128)}) custom-call(s32[1]{0:T(128)} %bitcast.mine_ref.refs_0_, s32[16]{0:T(128)} %refs_1_.5, bf16[16,176,128]{2,1,0:T(8,128)(2,1)} %copy-done, ...), custom_call_target="tpu_custom_call" | custom-call | tf_op jit(solution)/shard_map/step0/pallas_call | solution.py:328
  43.7 25.3 %all_to_all.20.refs_2_ = bf16[16,176,128]{2,1,0:T(8,128)(2,1)} all-to-all(bf16[16,176,128]{2,1,0:T(8,128)(2,1)} %get-tuple-element.31), channel_id=1, replica_groups=mesh['groups'=2,'tile'=16] {'tile'}, dimensions={0} | all-to-all | bytes 1441792 | tf_op jit(solution)/shard_map/all_to_all | solution.py:413
  69.0 13.4 %step1.1 = (f32[320,128]{1,0:T(8,128)}, f32[320,128]{1,0:T(8,128)}, f32[8,128]{1,0:T(8,128)}, bf16[16,176,128]{2,1,0:T(8,128)(2,1)}, f32[320,1024]{1,0:T(8,128)}) custom-call(s32[1]{0:T(128)} %bitcast.mine_ref.refs_0_, s32[16]{0:T(128)} %refs_1_.5, bf16[16,176,128]{2,1,0:T(8,128)(2,1)} %all_to_all.20.refs_2_, s32[16,128]{1,0:T(8,128)} %get-tuple-element.26.refs_3_, ...), custom_call_target="tpu_custom_call" | custom-call | tf_op jit(solution)/shard_map/step1/pallas_call | solution.py:328
  82.4 23.4 %all_to_all.21.refs_2_ = bf16[16,176,128]{2,1,0:T(8,128)(2,1)} all-to-all(bf16[16,176,128]{2,1,0:T(8,128)(2,1)} %get-tuple-element.36), channel_id=1, replica_groups=mesh['groups'=2,'tile'=16] {'tile'}, dimensions={0} | all-to-all | bytes 1441792 | tf_op jit(solution)/shard_map/all_to_all | solution.py:413
  105.8 12.9 %step2.1 = (f32[320,128]{1,0:T(8,128)}, f32[320,128]{1,0:T(8,128)}, f32[8,128]{1,0:T(8,128)}, f32[16,8,128]{2,1,0:T(8,128)}) custom-call(s32[1]{0:T(128)} %bitcast.mine_ref.refs_0_, s32[16]{0:T(128)} %refs_1_.5, bf16[16,176,128]{2,1,0:T(8,128)(2,1)} %all_to_all.21.refs_2_, s32[16,128]{1,0:T(8,128)} %get-tuple-element.26.refs_3_, ...), custom_call_target="tpu_custom_call" | custom-call | tf_op jit(solution)/shard_map/step2/pallas_call | solution.py:328
  118.7 11.0 %all_to_all.22.recv_ref = f32[16,8,128]{2,1,0:T(8,128)} all-to-all(f32[16,8,128]{2,1,0:T(8,128)} %get-tuple-element.40), channel_id=1, replica_groups=mesh['groups'=2,'tile'=16] {'tile'}, dimensions={0} | all-to-all | bytes 131072 | tf_op jit(solution)/shard_map/all_to_all | solution.py:413
  129.7 2.2 %last.1 = (f32[4,320,128]{2,1,0:T(8,128)}, f32[4,3]{1,0:T(4,128)}) custom-call(f32[16,8,128]{2,1,0:T(8,128)} %all_to_all.22.recv_ref, f32[8,128]{1,0:T(8,128)} %get-tuple-element.41.refs_0_, f32[8,128]{1,0:T(8,128)} %get-tuple-element.42.refs_1_, f32[8,128]{1,0:T(8,128)} %get-tuple-element.43.refs_2_, f32[320,128]{1,0:T(8,128)} %get-tuple-element.33.refs_8_.refs_3_, ...), custom_call_target="tpu_custom_call" | custom-call | tf_op jit(solution)/shard_map/last/pallas_call | solution.py:328
Async XLA Ops:
  3.4 26.6 %all-to-all-start = ((bf16[16,176,128]{2,1,0:T(8,128)(2,1)}), bf16[16,176,128]{2,1,0:T(8,128)(2,1)S(1)}, u32[]{:S(2)}, u32[]{:S(2)}) async-start(bf16[16,176,128]{2,1,0:T(8,128)(2,1)} %get-tuple-element.25), calls=%async_computation | async-start | bytes 1441792 | tf_op jit(solution)/shard_map/all_to_all | solution.py:369
  30.0 0.9 copy-start

commit v3 on v2

--- a/solution.py
+++ b/solution.py
@@ -12,7 +12,7 @@
 GROUP = 4
 F32 = jnp.float32
 BF16 = jnp.bfloat16
-VMEM_LIMIT = 56 * 1024 * 1024
+VMEM_LIMIT = 28 * 1024 * 1024
 
 
 def iota(shape, dim):
@@ -146,16 +146,8 @@
 
 
 def tables_kernel(sh, mine_ref, counts_ref, target_ref, offset_ref, tmatrix_ref, lattice_ref,
-                  pairs_ref, flipped_ref, turned_ref, code_ref, lattice_vmem, sems):
+                  pairs_ref, flipped_ref, turned_ref, code_ref):
     groups = sh.noff // GROUP
-    loads = [
-        pltpu.make_async_copy(
-            lattice_ref.at[pl.ds(g * GROUP, GROUP)], lattice_vmem.at[pl.ds(g * GROUP, GROUP)], sems.at[g]
-        )
-        for g in range(groups)
-    ]
-    for load in loads:
-        load.start()
     count = counts_ref[mine_ref[0]]
     code_ref[...] = wrap(target_ref[...], count) * sh.noff + offset_ref[...]
     eye = identity(sh.cap)
@@ -172,8 +164,7 @@
     wide = identity(sh.width)
     turned_ref[...] = dot_nt(wide, tmatrix_ref[...]).astype(BF16)
     for g in range(groups):
-        loads[g].wait()
-        some = lattice_vmem[g * GROUP : (g + 1) * GROUP].reshape(GROUP * sh.width, sh.width)
+        some = lattice_ref[g * GROUP : (g + 1) * GROUP].reshape(GROUP * sh.width, sh.width)
         span = GROUP * sh.width
         flipped_ref[:, g * span : (g + 1) * span] = dot_nt(wide, some).astype(BF16)
 
@@ -200,17 +191,9 @@
     last = step == ITERS - 1
     copy_out = None if last else take(1)[0]
     key_out = take(0 if step else 1)
-    flipped_vmem, sems, x_ref, p_ref = refs
+    x_ref, p_ref = refs
     groups = sh.noff // GROUP
     span = GROUP * sh.width
-    loads = [
-        pltpu.make_async_copy(
-            flipped_ref.at[:, pl.ds(g * span, span)], flipped_vmem.at[:, pl.ds(g * span, span)], sems.at[g]
-        )
-        for g in range(groups)
-    ]
-    for load in loads:
-        load.start()
     mine = mine_ref[0]
     count = counts_ref[mine]
     extras = jnp.zeros((16, LANES), F32)
@@ -269,8 +252,7 @@
                 p_ref[sh.cap + a : sh.cap + a + LANES, cols] = flag(key_ref[a : a + LANES, :] == float(o))
         summed = dot(x_ref[...], p_ref[...]).astype(BF16)
         stack = jnp.concatenate([summed[:, q * sh.cap : (q + 1) * sh.cap] for q in range(GROUP)], axis=0)
-        loads[g].wait()
-        field = field + dot(flipped_vmem[:, g * span : (g + 1) * span], stack)
+        field = field + dot(flipped_ref[:, g * span : (g + 1) * span], stack)
     live = (iota((1, sh.cap), 1) < count).astype(F32)
     image = live * dot(turned_ref[...], field.astype(BF16))
     image_out[...] = image
@@ -319,21 +301,25 @@
     basis_ref[ITERS] = next_vector(ITERS, image_ref[...], olds, sums)
 
 
-def call(kernel, name, outs, args, smem=0, hbm=(), scratch=()):
+def call(kernel, name, outs, args, smem=0, out_hbm=(), scratch=()):
     whole = pl.BlockSpec(memory_space=pltpu.VMEM)
-    specs = [
-        pl.BlockSpec(memory_space=pltpu.SMEM if i < smem else pl.ANY) if i < smem or i in hbm else whole
-        for i in range(len(args))
-    ]
+    specs, placed = [], []
+    for i, arg in enumerate(args):
+        space = pltpu.SMEM if i < smem else pltpu.VMEM
+        specs.append(pl.BlockSpec(memory_space=space))
+        placed.append(pltpu.with_memory_space_constraint(arg, space) if space is pltpu.VMEM else arg)
     return pl.pallas_call(
         kernel,
         name=name,
-        out_shape=[jax.ShapeDtypeStruct(shape, dtype) for shape, dtype in outs],
+        out_shape=[
+            jax.ShapeDtypeStruct(shape, dtype) if i in out_hbm else pltpu.VMEM(shape, dtype)
+            for i, (shape, dtype) in enumerate(outs)
+        ],
         in_specs=specs,
         out_specs=[whole] * len(outs),
         scratch_shapes=list(scratch),
         compiler_params=pltpu.CompilerParams(vmem_limit_bytes=VMEM_LIMIT),
-    )(*args)
+    )(*placed)
 
 
 def per_device(
@@ -350,7 +336,6 @@
     tiles = lax.axis_size("tile")
     cap, width = rhs.shape
     noff = lattice.shape[0]
-    groups = noff // GROUP
     sh = Shape(tiles, cap, width, local_target.shape[1], remote_tile.shape[1], noff)
     mine = lax.axis_index("tile").astype(jnp.int32).reshape(1)
     exchange = functools.partial(
@@ -373,12 +358,7 @@
         [((noff, cap, cap), BF16), ((width, noff * width), BF16), ((width, width), BF16)],
         [mine, counts, local_target.T, local_offset.T, tmatrix, lattice],
         smem=2,
-        hbm=(5,),
-        scratch=[
-            pltpu.VMEM((sh.nl, cap), jnp.int32),
-            pltpu.VMEM((noff, width, width), BF16),
-            pltpu.SemaphoreType.DMA((groups,)),
-        ],
+        scratch=[pltpu.VMEM((sh.nl, cap), jnp.int32)],
     )
     current, olds, copies, keys, seen = start, [], [], [], []
     for step in range(ITERS):
@@ -395,10 +375,7 @@
             outs,
             [mine, counts, recv, rank, pairs, turned, flipped, current, *olds, *copies, *keys],
             smem=2,
-            hbm=(6,),
             scratch=[
-                pltpu.VMEM((width, noff * width), BF16),
-                pltpu.SemaphoreType.DMA((groups,)),
                 pltpu.VMEM((width, sh.sources), BF16),
                 pltpu.VMEM((sh.sources, GROUP * cap), BF16),
             ],
@@ -416,6 +393,7 @@
         "last",
         [((ITERS + 1, width, cap), F32), ((ITERS + 1, ITERS), F32)],
         [recv, *seen, *olds, current],
+        out_hbm=(0, 1),
     )
     return jnp.transpose(basis, (0, 2, 1)), hess
 

time: 133 us -> 124 us (0.932)
  Pallas kernels: 63.3 us -> 41.8 us
  local copies, waits for them, and re-layouts: 0.87 us -> 15.4 us
  blocking collectives: 59.7 us -> 57.9 us
    pallas_call x6, Pallas kernels: 63.3 us -> 41.8 us  [call(): pl.pallas_call(kernel, name=name, out_shape=[jax.ShapeDtypeStruct(shape,...]
    unnamed x2 -> x28, local copies, waits for them, and re-layouts: 0.87 us -> 15.4 us
    all_to_all x3, blocking collectives: 59.7 us -> 57.9 us  [per_device(): recv = exchange(send)]
  transfers between devices with their start and end apart: 1 -> 1, of which waited for: 0 -> 0; matrix products, arithmetic and copies ran while one was open for 0% -> 0% of each run, Pallas kernels for 15% -> 11%
where the time goes in v3:
time: 124 us; the launch traced here: 123 us
  blocking collectives  57.9 us (47%)
  Pallas kernels  41.8 us (34%)
  local copies, waits for them, and re-layouts  15.4 us (12%)
  starting transfers between devices  7.36 us (6%)
    all_to_all x3, blocking collectives, per_device(): recv = exchange(send)  57.9 us
    pallas_call x6, Pallas kernels, call(): pl.pallas_call(kernel, name=name, out_shape=[jax.ShapeDtypeStruct(shape,...  41.8 us
    unnamed x28, local copies, waits for them, and re-layouts  15.4 us
    all_to_all x1, starting transfers between devices, per_device(): recv = exchange(send)  7.36 us
  transfers between devices with their start and end apart: 1, of which 0 were waited for; matrix products, arithmetic and copies ran while one was open for 0% of the time, Pallas kernels for 11%

profile of v3, /device:TPU:0, one launch (start us, length us, event | category | flops | bytes accessed | tf_op | source)
XLA Modules:
  0.0 123.1 jit_solution(715317129592271396)
XLA Ops:
  0.6 0.0 copy-start.8
  0.6 0.0 copy-start.5
  0.7 0.9 copy-done.5
  1.6 0.0 copy-start.6
  1.6 0.7 copy-done.6
  2.2 0.0 copy-start.11
  2.2 0.7 copy-done.11
  2.9 0.0 copy-start.12
  2.9 0.7 copy-done.12
  3.6 0.0 copy-start.13
  3.6 0.7 copy-done.13
  4.3 2.3 %first.1 = (f32[320,128]{1,0:T(8,128)S(1)}, s32[16,128]{1,0:T(8,128)S(1)}, bf16[16,176,128]{2,1,0:T(8,128)(2,1)}) custom-call(s32[1]{0:T(128)} %bitcast.mine_ref.refs_0_, s32[16]{0:T(128)S(1)} %copy-done.6, f32[320,128]{1,0:T(8,128)S(1)} %bitcast.8, s32[4,128]{1,0:T(4,128)S(1)} %bitcast.11, s32[4,128]{1,0:T(4,128)S(1)} %bitcast.12, s32[4,128]{1,0:T(4,128)S(1)} %bitcast.13), custom_call_target="tpu_custom_call" | custom-call | tf_op jit(solution)/shard_map/first/pallas_call | solution.py:311
  6.6 7.4 %all-to-all-start = ((bf16[16,176,128]{2,1,0:T(8,128)(2,1)}), bf16[16,176,128]{2,1,0:T(8,128)(2,1)S(1)}, u32[]{:S(2)}, u32[]{:S(2)}) async-start(bf16[16,176,128]{2,1,0:T(8,128)(2,1)} %get-tuple-element.25), calls=%async_computation | async-start | bytes 1441792 | tf_op jit(solution)/shard_map/all_to_all | solution.py:354
  13.9 0.0 copy-start.3
  13.9 3.2 %copy-done.3 = bf16[32,320,320]{2,1,0:T(8,128)(2,1)S(1)} copy-done((bf16[32,320,320]{2,1,0:T(8,128)(2,1)S(1)}, bf16[32,320,320]{2,1,0:T(8,128)(2,1)}, u32[]{:S(2)}) %copy-start.3) | copy-done | bytes 6553624
  17.2 0.0 copy-start.4
  17.2 0.9 copy-done.4
  18.1 0.0 copy-start.7
  18.1 0.7 copy-done.7
  18.8 0.0 copy-start.9
  18.8 0.7 copy-done.9
  19.5 0.0 copy-start.10
  19.5 0.7 copy-done.10
  20.2 13.7 %tables.1 = (bf16[32,128,128]{2,1,0:T(8,128)(2,1)S(1)}, bf16[320,10240]{1,0:T(8,128)(2,1)S(1)}, bf16[320,320]{1,0:T(8,128)(2,1)S(1)}) custom-call(s32[1]{0:T(128)} %bitcast.mine_ref.refs_0_, s32[16]{0:T(128)S(1)} %copy-done.7, s32[24,128]{1,0:T(8,128)S(1)} %bitcast.9, s32[24,128]{1,0:T(8,128)S(1)} %bitcast.10, bf16[320,320]{1,0:T(8,128)(2,1)S(1)} %copy-done.4, ...), custom_call_target="tpu_custom_call" | custom-call | tf_op jit(solution)/shard_map/tables/pallas_call | solution.py:311
  33.9 0.0 copy-start
  33.9 2.7 %copy-done = bf16[320,10240]{1,0:T(8,128)(2,1)} copy-done((bf16[320,10240]{1,0:T(8,128)(2,1)}, bf16[320,10240]{1,0:T(8,128)(2,1)S(1)}, u32[]{:S(2)}) %copy-start) | copy-done | bytes 6553624
  36.6 0.0 all-to-all-done.refs_2_
  36.6 0.0 copy-done.8
  36.6 0.0 copy-start.1
  36.6 2.9 %copy-done.1 = bf16[320,10240]{1,0:T(8,128)(2,1)S(1)} copy-done((bf16[320,10240]{1,0:T(8,128)(2,1)S(1)}, bf16[320,10240]{1,0:T(8,128)(2,1)}, u32[]{:S(2)}) %copy-start.1) | copy-done | bytes 6553624
  39.5 0.0 copy-start.2
  39.5 8.5 %step0.1 = (f32[320,128]{1,0:T(8,128)S(1)}, f32[320,128]{1,0:T(8,128)S(1)}, f32[8,128]{1,0:T(8,128)S(1)}, bf16[16,176,128]{2,1,0:T(8,128)(2,1)S(1)}, f32[320,1024]{1,0:T(8,128)S(1)}, /*index=5*/f32[1024,128]{1,0:T(8,128)S(1)}) custom-call(s32[1]{0:T(128)} %bitcast.mine_ref.refs_0_, s32[16]{0:T(128)S(1)} %copy-done.8, ...), custom_call_target="tpu_custom_call" | custom-call | tf_op jit(solution)/shard_map/step0/pallas_call | solution.py:311
  48.0 24.9 %all_to_all.20.refs_2_ = bf16[16,176,128]{2,1,0:T(8,128)(2,1)S(1)} all-to-all(bf16[16,176,128]{2,1,0:T(8,128)(2,1)S(1)} %get-tuple-element.31), channel_id=1, replica_groups=mesh['groups'=2,'tile'=16] {'tile'}, dimensions={0} | all-to-all | bytes 1441792 | tf_op jit(solution)/shard_map/all_to_all | solution.py:390
  72.9 0.0 copy-done.2
  72.9 8.4 %step1.1 = (f32[320,128]{1,0:T(8,128)S(1)}, f32[320,128]{1,0:T(8,128)S(1)}, f32[8,128]{1,0:T(8,128)S(1)}, bf16[16,176,128]{2,1,0:T(8,128)(2,1)S(1)}, f32[320,1024]{1,0:T(8,128)S(1)}) custom-call(s32[1]{0:T(128)} %bitcast.mine_ref.refs_0_, s32[16]{0:T(128)S(1)} %copy-done.8, bf16[16,176,128]{2,1,0:T(8,128)(2,1)S(1)} %all_to_all.20.refs_2_, ...), custom_call_target="tpu_custom_call" | custom-call | tf_op jit(solution)/shard_map/step1/pallas_call | solution.py:311
  81.3 22.6 %all_to_all.21.refs_2_ = bf16[16,176,128]{2,1,0:T(8,128)(2,1)S(1)} all-to-all(bf16[16,176,128]{2,1,0:T(8,128)(2,1)S(1)} %get-tuple-element.36), channel_id=1, replica_groups=mesh['groups'=2,'tile'=16] {'tile'}, dimensions={0} | all-to-all | bytes 1441792 | tf_op jit(solution)/shard_map/all_to_all | solution.py:390
  103.9 7.9 %step2.1 = (f32[320,128]{1,0:T(8,128)S(1)}, f32[320,128]{1,0:T(8,128)S(1)}, f32[8,128]{1,0:T(8,128)S(1)}, f32[16,8,128]{2,1,0:T(8,128)S(1)}) custom-call(s32[1]{0:T(128)} %bitcast.mine_ref.refs_0_, s32[16]{0:T(128)S(1)} %copy-done.8, bf16[16,176,128]{2,1,0:T(8,128)(2,1)S(1)} %all_to_all.21.refs_2_, s32[16,128]{1,0:T(8,128)S(1)} %get-tuple-element.26.refs_3_, ...), custom_call_target="tpu_custom_call" | custom-call | tf_op jit(solution)/shard_map/step2/pallas_call | solution.py:311
  111.8 10.3 %all_to_all.22.recv_ref = f32[16,8,128]{2,1,0:T(8,128)S(1)} all-to-all(f32[16,8,128]{2,1,0:T(8,128)S(1)} %get-tuple-element.40), channel_id=1, replica_groups=mesh['groups'=2,'tile'=16] {'tile'}, dimensions={0} | all-to-all | bytes 131072 | tf_op jit(solution)/shard_map/all_to_all | solution.py:390
  122.1 1.0 last.1
Async XLA Ops:
  0.6 36.0 %copy-start.8 = (s32[16]{0:T(128)S(1)}, s32[16]{0:T(128)}, u32[]{:S(2)}) copy-start(s32[16]{0:T(128)} %refs_1_.5) | copy-start | bytes 196
  0.6 0.9 copy-start.5
  1.6 0.7 copy-start.6
  2.2 0.7 copy-start.11
  2.9 0.7 copy-start.12
  3.6 0.7 copy-start.13
  6.6 30.1 %all-to-all-start = ((bf16[16,176,128]{2,1,0:T(8,128)(2,1)}), bf16[16,176,128]{2,1,0:T(8,128)(2,1)S(1)}, u32[]{:S(2)}, u32[]{:S(2)}) async-start(bf16[16,176,128]{2,1,0:T(8,128)(2,1)} %get-tuple-element.25), calls=%async_computation | async-start | bytes 1441792 | tf_op jit(solution)/shard_map/all_to_all | solution.py:354
  13.9 3.2 %copy-start.3 = (bf16[32,320,320]{2,1,0:T(8,128)(2,1)S(1)}, bf16[32,320,320]{2,1,0:T(8,128)(2,1)}, u32[]{:S(2)}) copy-start(bf16[32,320,320]{2,1,0:T(8,128)(2,1)} %lattice_ref.1) | copy-start | bytes 19660804
  17.2 0.9 copy-start.4
  18.1 0.7 copy-start.7
  18.8 0.7 copy-start.9
  19.5 0.7 copy-start.10
  33.9 2.7 %copy-start = (bf16[320,10240]{1,0:T(8,128)(2,1)}, bf16[320,10240]{1,0:T(8,128)(2,1)S(1)}, u32[]{:S(2)}) copy-start(bf16[320,10240]{1,0:T(8,128)(2,1)S(1)} %get-tuple-element.29.refs_6_) | copy-start | bytes 19660804
  36.6 2.9 %copy-start.1 = (bf16[320,10240]{1,0:T(8,128)(2,1)S(1)}, bf16[320,10240]{1,0:T(8,128)(2,1)}, u32[]{:S(2)}) copy-start(bf16[320,10240]{1,0:T(8,128)(2,1)} %copy-done) | copy-start | bytes 19660804
  39.5 33.4 %copy-start.2 = (bf16[320,10240]{1,0:T(8,128)(2,1)S(1)}, bf16[320,10240]{1,0:T(8,128)(2,1)}, u32[]{:S(2)}) copy-start(bf16[320,10240]{1,0:T(8,128)(2,1)} %copy-done) | copy-start | bytes 19660804

commit v4 on v3

--- a/solution.py
+++ b/solution.py
@@ -146,8 +146,16 @@
 
 
 def tables_kernel(sh, mine_ref, counts_ref, target_ref, offset_ref, tmatrix_ref, lattice_ref,
-                  pairs_ref, flipped_ref, turned_ref, code_ref):
+                  pairs_ref, flipped_ref, turned_ref, code_ref, lattice_vmem, sems):
     groups = sh.noff // GROUP
+    loads = [
+        pltpu.make_async_copy(
+            lattice_ref.at[pl.ds(g * GROUP, GROUP)], lattice_vmem.at[pl.ds(g * GROUP, GROUP)], sems.at[g]
+        )
+        for g in range(groups)
+    ]
+    for load in loads:
+        load.start()
     count = counts_ref[mine_ref[0]]
     code_ref[...] = wrap(target_ref[...], count) * sh.noff + offset_ref[...]
     eye = identity(sh.cap)
@@ -164,7 +172,8 @@
     wide = identity(sh.width)
     turned_ref[...] = dot_nt(wide, tmatrix_ref[...]).astype(BF16)
     for g in range(groups):
-        some = lattice_ref[g * GROUP : (g + 1) * GROUP].reshape(GROUP * sh.width, sh.width)
+        loads[g].wait()
+        some = lattice_vmem[g * GROUP : (g + 1) * GROUP].reshape(GROUP * sh.width, sh.width)
         span = GROUP * sh.width
         flipped_ref[:, g * span : (g + 1) * span] = dot_nt(wide, some).astype(BF16)
 
@@ -191,7 +200,7 @@
     last = step == ITERS - 1
     copy_out = None if last else take(1)[0]
     key_out = take(0 if step else 1)
-    x_ref, p_ref = refs
+    x_ref = refs[0]
     groups = sh.noff // GROUP
     span = GROUP * sh.width
     mine = mine_ref[0]
@@ -220,7 +229,9 @@
             empty = 1.0 - table[2:3]
             table = jnp.where(row == 0, target, table)
             table = jnp.where(row == 3, empty, jnp.where(row > 3, 0.0, table))
-            key_ref[c * LANES : (c + 1) * LANES, :] = dot_tn(table.astype(BF16), weight)
+            key = dot_tn(table.astype(BF16), weight)
+            key = jnp.where((key >= 0.0) & (key < sh.noff), key, -1.0)
+            key_ref[c * LANES : (c + 1) * LANES, :] = key.astype(BF16)
     else:
         key_ref = key_in[0]
     lane_group = iota((1, LANES), 1) // sh.slots
@@ -242,15 +253,13 @@
             copy_out[:, a : a + LANES] = column
         x_ref[:, sh.cap + a : sh.cap + a + LANES] = column.astype(BF16)
     field = jnp.zeros((sh.width, sh.cap), F32)
+    one, zero = jnp.ones((), BF16), jnp.zeros((), BF16)
     for g in range(groups):
-        for q in range(GROUP):
-            o = g * GROUP + q
-            cols = slice(q * sh.cap, (q + 1) * sh.cap)
-            p_ref[0 : sh.cap, cols] = pairs_ref[o]
-            for c in range(sh.chunks):
-                a = c * LANES
-                p_ref[sh.cap + a : sh.cap + a + LANES, cols] = flag(key_ref[a : a + LANES, :] == float(o))
-        summed = dot(x_ref[...], p_ref[...]).astype(BF16)
+        counts_of = []
+        for o in range(g * GROUP, (g + 1) * GROUP):
+            hits = jnp.where(key_ref[...] == jnp.asarray(o, BF16), one, zero)
+            counts_of.append(jnp.concatenate([pairs_ref[o], hits], axis=0))
+        summed = dot(x_ref[...], jnp.concatenate(counts_of, axis=1)).astype(BF16)
         stack = jnp.concatenate([summed[:, q * sh.cap : (q + 1) * sh.cap] for q in range(GROUP)], axis=0)
         field = field + dot(flipped_ref[:, g * span : (g + 1) * span], stack)
     live = (iota((1, sh.cap), 1) < count).astype(F32)
@@ -301,13 +310,14 @@
     basis_ref[ITERS] = next_vector(ITERS, image_ref[...], olds, sums)
 
 
-def call(kernel, name, outs, args, smem=0, out_hbm=(), scratch=()):
+def call(kernel, name, outs, args, smem=0, plain=False, hbm=(), out_hbm=(), scratch=()):
     whole = pl.BlockSpec(memory_space=pltpu.VMEM)
     specs, placed = [], []
     for i, arg in enumerate(args):
-        space = pltpu.SMEM if i < smem else pltpu.VMEM
+        space = pltpu.SMEM if i < smem else pl.ANY if i in hbm else pltpu.VMEM
         specs.append(pl.BlockSpec(memory_space=space))
-        placed.append(pltpu.with_memory_space_constraint(arg, space) if space is pltpu.VMEM else arg)
+        held = pltpu.HBM if i < smem or plain else pltpu.VMEM
+        placed.append(pltpu.with_memory_space_constraint(arg, held))
     return pl.pallas_call(
         kernel,
         name=name,
@@ -349,6 +359,7 @@
         [own, ((tiles, cap), jnp.int32), block],
         [mine, counts, rhs.T, remote_tile.T, remote_target.T, remote_offset.T],
         smem=2,
+        plain=True,
         scratch=[pltpu.VMEM((3, tiles, cap), F32)],
     )
     recv = exchange(send)
@@ -358,7 +369,13 @@
         [((noff, cap, cap), BF16), ((width, noff * width), BF16), ((width, width), BF16)],
         [mine, counts, local_target.T, local_offset.T, tmatrix, lattice],
         smem=2,
-        scratch=[pltpu.VMEM((sh.nl, cap), jnp.int32)],
+        plain=True,
+        hbm=(5,),
+        scratch=[
+            pltpu.VMEM((sh.nl, cap), jnp.int32),
+            pltpu.VMEM((noff, width, width), BF16),
+            pltpu.SemaphoreType.DMA((noff // GROUP,)),
+        ],
     )
     current, olds, copies, keys, seen = start, [], [], [], []
     for step in range(ITERS):
@@ -368,17 +385,14 @@
         if not last:
             outs.append(((width, sh.inbound), F32))
         if step == 0:
-            outs.append(((sh.inbound, LANES), F32))
+            outs.append(((sh.inbound, LANES), BF16))
         result = call(
             functools.partial(step_kernel, sh, step),
             f"step{step}",
             outs,
             [mine, counts, recv, rank, pairs, turned, flipped, current, *olds, *copies, *keys],
             smem=2,
-            scratch=[
-                pltpu.VMEM((width, sh.sources), BF16),
-                pltpu.VMEM((sh.sources, GROUP * cap), BF16),
-            ],
+            scratch=[pltpu.VMEM((width, sh.sources), BF16)],
         )
         vector, current, sums, send = result[:4]
         olds.append(vector)

time: 124 us -> 116 us (0.935)
  local copies, waits for them, and re-layouts: 15.4 us -> 5.59 us
  Pallas kernels: 41.8 us -> 44 us
    unnamed x28 -> x6, local copies, waits for them, and re-layouts: 15.4 us -> 5.59 us
    pallas_call x6, Pallas kernels: 41.8 us -> 44 us  [call(): pl.pallas_call(kernel, name=name, out_shape=[jax.ShapeDtypeStruct(shape,...]
  transfers between devices with their start and end apart: 1 -> 1, of which waited for: 0 -> 0; matrix products, arithmetic and copies ran while one was open for 0% -> 0% of each run, Pallas kernels for 11% -> 14%
where the time goes in v4:
time: 116 us; the launch traced here: 115 us
  blocking collectives  57.9 us (50%)
  Pallas kernels  44 us (38%)
  starting transfers between devices  7.36 us (6%)
  local copies, waits for them, and re-layouts  5.59 us (5%)
    all_to_all x3, blocking collectives, per_device(): recv = exchange(send)  57.9 us
    pallas_call x6, Pallas kernels, call(): pl.pallas_call(kernel, name=name, out_shape=[jax.ShapeDtypeStruct(shape,...  44 us
    all_to_all x1, starting transfers between devices, per_device(): recv = exchange(send)  7.36 us
    unnamed x6, local copies, waits for them, and re-layouts  5.59 us
  transfers between devices with their start and end apart: 1, of which 0 were waited for; matrix products, arithmetic and copies ran while one was open for 0% of the time, Pallas kernels for 14%

profile of v4, /device:TPU:0, one launch (start us, length us, event | category | flops | bytes accessed | tf_op | source)
XLA Modules:
  0.0 115.5 jit_solution(831467716851484703)
XLA Ops:
  0.6 2.7 %first.1 = (f32[320,128]{1,0:T(8,128)S(1)}, s32[16,128]{1,0:T(8,128)S(1)}, bf16[16,176,128]{2,1,0:T(8,128)(2,1)}) custom-call(s32[1]{0:T(128)} %bitcast.mine_ref.refs_0_, s32[16]{0:T(128)} %refs_1_.5, f32[320,128]{1,0:T(8,128)} %bitcast.8, s32[4,128]{1,0:T(4,128)} %bitcast.11, s32[4,128]{1,0:T(4,128)} %bitcast.12, s32[4,128]{1,0:T(4,128)} %bitcast.13), custom_call_target="tpu_custom_call" | custom-call | tf_op jit(solution)/shard_map/first/pallas_call | solution.py:321
  3.4 7.4 %all-to-all-start = ((bf16[16,176,128]{2,1,0:T(8,128)(2,1)}), bf16[16,176,128]{2,1,0:T(8,128)(2,1)S(1)}, u32[]{:S(2)}, u32[]{:S(2)}) async-start(bf16[16,176,128]{2,1,0:T(8,128)(2,1)} %get-tuple-element.25), calls=%async_computation | async-start | bytes 1441792 | tf_op jit(solution)/shard_map/all_to_all | solution.py:365
  10.7 16.5 %tables.1 = (bf16[32,128,128]{2,1,0:T(8,128)(2,1)S(1)}, bf16[320,10240]{1,0:T(8,128)(2,1)S(1)}, bf16[320,320]{1,0:T(8,128)(2,1)S(1)}) custom-call(s32[1]{0:T(128)} %bitcast.mine_ref.refs_0_, s32[16]{0:T(128)} %refs_1_.5, s32[24,128]{1,0:T(8,128)} %bitcast.9, s32[24,128]{1,0:T(8,128)} %bitcast.10, bf16[320,320]{1,0:T(8,128)(2,1)} %tmatrix_ref.1, ...), custom_call_target="tpu_custom_call" | custom-call | tf_op jit(solution)/shard_map/tables/pallas_call | solution.py:321
  27.2 0.0 copy-start
  27.2 2.7 %copy-done = bf16[320,10240]{1,0:T(8,128)(2,1)} copy-done((bf16[320,10240]{1,0:T(8,128)(2,1)}, bf16[320,10240]{1,0:T(8,128)(2,1)S(1)}, u32[]{:S(2)}) %copy-start) | copy-done | bytes 6553624
  30.0 0.0 all-to-all-done.refs_2_
  30.0 0.0 copy-start.1
  30.0 2.9 %copy-done.1 = bf16[320,10240]{1,0:T(8,128)(2,1)S(1)} copy-done((bf16[320,10240]{1,0:T(8,128)(2,1)S(1)}, bf16[320,10240]{1,0:T(8,128)(2,1)}, u32[]{:S(2)}) %copy-start.1) | copy-done | bytes 6553624
  32.8 0.0 copy-start.2
  32.8 8.3 %step0.1 = (f32[320,128]{1,0:T(8,128)S(1)}, f32[320,128]{1,0:T(8,128)S(1)}, f32[8,128]{1,0:T(8,128)S(1)}, bf16[16,176,128]{2,1,0:T(8,128)(2,1)S(1)}, f32[320,102...) custom-call(s32[1]{0:T(128)} %bitcast.mine_ref.refs_0_, s32[16]{0:T(128)} %refs_1_.5, ...), custom_call_target="tpu_custom_call" | custom-call | tf_op jit(solution)/shard_map/step0/pallas_call | solution.py:321
  41.1 24.9 %all_to_all.20.refs_2_ = bf16[16,176,128]{2,1,0:T(8,128)(2,1)S(1)} all-to-all(bf16[16,176,128]{2,1,0:T(8,128)(2,1)S(1)} %get-tuple-element.31), channel_id=1, replica_groups=mesh['groups'=2,'tile'=16] {'tile'}, dimensions={0} | all-to-all | bytes 1441792 | tf_op jit(solution)/shard_map/all_to_all | solution.py:404
  66.0 0.0 copy-done.2
  66.0 8.0 %step1.1 = (f32[320,128]{1,0:T(8,128)S(1)}, f32[320,128]{1,0:T(8,128)S(1)}, f32[8,128]{1,0:T(8,128)S(1)}, bf16[16,176,128]{2,1,0:T(8,128)(2,1)S(1)}, f32[320,1024]{1,0:T(8,128)S(1)}) custom-call(s32[1]{0:T(128)} %bitcast.mine_ref.refs_0_, s32[16]{0:T(128)} %refs_1_.5, bf16[16,176,128]{2,1,0:T(8,128)(2,1)S(1)} %all_to_all.20.refs_2_, ...), custom_call_target="tpu_custom_call" | custom-call | tf_op jit(solution)/shard_map/step1/pallas_call | solution.py:321
  74.0 22.6 %all_to_all.21.refs_2_ = bf16[16,176,128]{2,1,0:T(8,128)(2,1)S(1)} all-to-all(bf16[16,176,128]{2,1,0:T(8,128)(2,1)S(1)} %get-tuple-element.36), channel_id=1, replica_groups=mesh['groups'=2,'tile'=16] {'tile'}, dimensions={0} | all-to-all | bytes 1441792 | tf_op jit(solution)/shard_map/all_to_all | solution.py:404
  96.6 7.5 %step2.1 = (f32[320,128]{1,0:T(8,128)S(1)}, f32[320,128]{1,0:T(8,128)S(1)}, f32[8,128]{1,0:T(8,128)S(1)}, f32[16,8,128]{2,1,0:T(8,128)S(1)}) custom-call(s32[1]{0:T(128)} %bitcast.mine_ref.refs_0_, s32[16]{0:T(128)} %refs_1_.5, bf16[16,176,128]{2,1,0:T(8,128)(2,1)S(1)} %all_to_all.21.refs_2_, s32[16,128]{1,0:T(8,128)S(1)} %get-tuple-element.26.refs_3_, ...), custom_call_target="tpu_custom_call" | custom-call | tf_op jit(solution)/shard_map/step2/pallas_call | solution.py:321
  104.1 10.3 %all_to_all.22.recv_ref = f32[16,8,128]{2,1,0:T(8,128)S(1)} all-to-all(f32[16,8,128]{2,1,0:T(8,128)S(1)} %get-tuple-element.40), channel_id=1, replica_groups=mesh['groups'=2,'tile'=16] {'tile'}, dimensions={0} | all-to-all | bytes 131072 | tf_op jit(solution)/shard_map/all_to_all | solution.py:404
  114.5 1.0 last.1
Async XLA Ops:
  3.4 26.6 %all-to-all-start = ((bf16[16,176,128]{2,1,0:T(8,128)(2,1)}), bf16[16,176,128]{2,1,0:T(8,128)(2,1)S(1)}, u32[]{:S(2)}, u32[]{:S(2)}) async-start(bf16[16,176,128]{2,1,0:T(8,128)(2,1)} %get-tuple-element.25), calls=%async_computation | async-start | bytes 1441792 | tf_op jit(solution)/shard_map/all_to_all | solution.py:365
  27.2 2.7 %copy-start = (bf16[320,10240]{1,0:T(8,128)(2,1)}, bf16[320,10240]{1,0:T(8,128)(2,1)S(1)}, u32[]{:S(2)}) copy-start(bf16[320,10240]{1,0:T(8,128)(2,1)S(1)} %get-tuple-element.29.refs_6_) | copy-start | bytes 19660804
  30.0 2.9 %copy-start.1 = (bf16[320,10240]{1,0:T(8,128)(2,1)S(1)}, bf16[320,10240]{1,0:T(8,128)(2,1)}, u32[]{:S(2)}) copy-start(bf16[320,10240]{1,0:T(8,128)(2,1)} %copy-done) | copy-start | bytes 19660804
  32.8 33.2 %copy-start.2 = (bf16[320,10240]{1,0:T(8,128)(2,1)S(1)}, bf16[320,10240]{1,0:T(8,128)(2,1)}, u32[]{:S(2)}) copy-start(bf16[320,10240]{1,0:T(8,128)(2,1)} %copy-done) | copy-start | bytes 19660804

commit v5 on v4

--- a/solution.py
+++ b/solution.py
@@ -10,6 +10,7 @@
 ITERS = 3
 LANES = 128
 GROUP = 4
+AHEAD = 2
 F32 = jnp.float32
 BF16 = jnp.bfloat16
 VMEM_LIMIT = 28 * 1024 * 1024
@@ -145,8 +146,26 @@
     each(sh.tiles, body)
 
 
-def tables_kernel(sh, mine_ref, counts_ref, target_ref, offset_ref, tmatrix_ref, lattice_ref,
-                  pairs_ref, flipped_ref, turned_ref, code_ref, lattice_vmem, sems):
+def slot_keys(sh, target, offset, empty):
+    rows = iota((16, target.shape[1]), 0)
+    table = jnp.where(rows == 0, target, 0.0)
+    table = jnp.where(rows == 1, offset, table)
+    table = jnp.where(rows == 2, 1.0, table)
+    if empty is not None:
+        table = jnp.where(rows == 3, empty, table)
+    row, col = iota((16, sh.cap), 0), iota((16, sh.cap), 1)
+    weight = jnp.where(row == 0, sh.noff, 0) + jnp.where(row == 1, 1, 0)
+    weight = weight - jnp.where(row == 2, col * sh.noff, 0) - jnp.where(row == 3, 16384, 0)
+    key = dot_tn(table.astype(BF16), weight.astype(F32).astype(BF16))
+    return jnp.where((key >= 0.0) & (key < sh.noff), key, -1.0).astype(BF16)
+
+
+def matches(keys, o):
+    return jnp.where(keys == o, jnp.ones((), BF16), jnp.zeros((), BF16))
+
+
+def tables_kernel(sh, mine_ref, counts_ref, target_ref, offset_ref, tmatrix_ref, lattice_ref, *refs):
+    pairs_ref, turned_ref, flipped_ref, key_ref, lattice_vmem, flipped_vmem, sems, out_sems = refs
     groups = sh.noff // GROUP
     loads = [
         pltpu.make_async_copy(
@@ -157,25 +176,27 @@
     for load in loads:
         load.start()
     count = counts_ref[mine_ref[0]]
-    code_ref[...] = wrap(target_ref[...], count) * sh.noff + offset_ref[...]
-    eye = identity(sh.cap)
-
-    def body(o, carry):
-        mark = iota((sh.cap, sh.cap), 0) * sh.noff + o
-        amount = jnp.zeros((sh.cap, sh.cap), F32)
-        for n in range(sh.nl):
-            amount = amount + (code_ref[n : n + 1, :] == mark).astype(F32)
-        pairs_ref[o] = dot_nt(eye, amount.astype(BF16)).astype(BF16)
-        return carry
-
-    lax.fori_loop(0, sh.noff, body, 0)
+    target = wrap(target_ref[...], count).astype(F32)
+    offset = offset_ref[...].astype(F32)
+    for n in range(sh.nl):
+        key_ref[n] = slot_keys(sh, target[n : n + 1, :], offset[n : n + 1, :], None)
+    for o in range(sh.noff):
+        amount = matches(key_ref[0], jnp.asarray(o, BF16))
+        for n in range(1, sh.nl):
+            amount = amount + matches(key_ref[n], jnp.asarray(o, BF16))
+        pairs_ref[o] = amount
     wide = identity(sh.width)
     turned_ref[...] = dot_nt(wide, tmatrix_ref[...]).astype(BF16)
+    span = GROUP * sh.width
+    stores = []
     for g in range(groups):
         loads[g].wait()
-        some = lattice_vmem[g * GROUP : (g + 1) * GROUP].reshape(GROUP * sh.width, sh.width)
-        span = GROUP * sh.width
-        flipped_ref[:, g * span : (g + 1) * span] = dot_nt(wide, some).astype(BF16)
+        some = lattice_vmem[g * GROUP : (g + 1) * GROUP].reshape(span, sh.width)
+        flipped_vmem[g] = dot_nt(wide, some).astype(BF16)
+        stores.append(pltpu.make_async_copy(flipped_vmem.at[g], flipped_ref.at[g], out_sems.at[g]))
+        stores[g].start()
+    for store in stores:
+        store.wait()
 
 
 def next_vector(step, current, olds, sums):
@@ -192,7 +213,8 @@
 def step_kernel(sh, step, *refs):
     refs = list(refs)
     take = lambda n: [refs.pop(0) for _ in range(n)]
-    mine_ref, counts_ref, recv_ref, rank_ref, pairs_ref, turned_ref, flipped_ref, current_ref = take(8)
+    mine_ref, counts_ref, recv_ref, rank_ref, pairs_ref, turned_ref = take(6)
+    flipped_ref, current_ref = take(2)
     olds = take(step)
     copies = take(step)
     key_in = take(1 if step else 0)
@@ -200,9 +222,15 @@
     last = step == ITERS - 1
     copy_out = None if last else take(1)[0]
     key_out = take(0 if step else 1)
-    x_ref = refs[0]
+    flipped_out = take(0 if step else 1)
+    x_ref, *sems = refs
     groups = sh.noff // GROUP
-    span = GROUP * sh.width
+    loads = []
+    if step == 0:
+        source, flipped_ref = flipped_ref, flipped_out[0]
+        loads = [pltpu.make_async_copy(source.at[g], flipped_ref.at[g], sems[0].at[g]) for g in range(groups)]
+    for load in loads[:AHEAD]:
+        load.start()
     mine = mine_ref[0]
     count = counts_ref[mine]
     extras = jnp.zeros((16, LANES), F32)
@@ -217,21 +245,12 @@
     x_ref[:, 0 : sh.cap] = vector.astype(BF16)
     if step == 0:
         key_ref = key_out[0]
-        row = iota((16, LANES), 0)
-        weight = jnp.where(row == 0, sh.noff, 0) + jnp.where(row == 1, 1, 0)
-        weight = weight - jnp.where(row == 2, iota((16, LANES), 1) * sh.noff, 0)
-        weight = (weight - jnp.where(row == 3, 16384, 0)).astype(F32).astype(BF16)
         for c in range(sh.chunks):
             table = jnp.zeros((16, LANES), F32)
             for s in range(c * sh.fold, (c + 1) * sh.fold):
                 table = table + recv_ref[s, sh.extra :, :].astype(F32)
             target = wrap(table[0:1].astype(jnp.int32), count).astype(F32)
-            empty = 1.0 - table[2:3]
-            table = jnp.where(row == 0, target, table)
-            table = jnp.where(row == 3, empty, jnp.where(row > 3, 0.0, table))
-            key = dot_tn(table.astype(BF16), weight)
-            key = jnp.where((key >= 0.0) & (key < sh.noff), key, -1.0)
-            key_ref[c * LANES : (c + 1) * LANES, :] = key.astype(BF16)
+            key_ref[c * LANES : (c + 1) * LANES, :] = slot_keys(sh, target, table[1:2], 1.0 - table[2:3])
     else:
         key_ref = key_in[0]
     lane_group = iota((1, LANES), 1) // sh.slots
@@ -253,15 +272,18 @@
             copy_out[:, a : a + LANES] = column
         x_ref[:, sh.cap + a : sh.cap + a + LANES] = column.astype(BF16)
     field = jnp.zeros((sh.width, sh.cap), F32)
-    one, zero = jnp.ones((), BF16), jnp.zeros((), BF16)
     for g in range(groups):
         counts_of = []
         for o in range(g * GROUP, (g + 1) * GROUP):
-            hits = jnp.where(key_ref[...] == jnp.asarray(o, BF16), one, zero)
+            hits = matches(key_ref[...], jnp.asarray(o, BF16))
             counts_of.append(jnp.concatenate([pairs_ref[o], hits], axis=0))
         summed = dot(x_ref[...], jnp.concatenate(counts_of, axis=1)).astype(BF16)
         stack = jnp.concatenate([summed[:, q * sh.cap : (q + 1) * sh.cap] for q in range(GROUP)], axis=0)
-        field = field + dot(flipped_ref[:, g * span : (g + 1) * span], stack)
+        if loads:
+            loads[g].wait()
+            if g + AHEAD < groups:
+                loads[g + AHEAD].start()
+        field = field + dot(flipped_ref[g], stack)
     live = (iota((1, sh.cap), 1) < count).astype(F32)
     image = live * dot(turned_ref[...], field.astype(BF16))
     image_out[...] = image
@@ -310,23 +332,24 @@
     basis_ref[ITERS] = next_vector(ITERS, image_ref[...], olds, sums)
 
 
-def call(kernel, name, outs, args, smem=0, plain=False, hbm=(), out_hbm=(), scratch=()):
-    whole = pl.BlockSpec(memory_space=pltpu.VMEM)
+def call(kernel, name, outs, args, smem=0, plain=False, hbm=(), out_hbm=(), out_plain=(), scratch=()):
     specs, placed = [], []
     for i, arg in enumerate(args):
         space = pltpu.SMEM if i < smem else pl.ANY if i in hbm else pltpu.VMEM
         specs.append(pl.BlockSpec(memory_space=space))
-        held = pltpu.HBM if i < smem or plain else pltpu.VMEM
+        held = pltpu.HBM if i < smem or plain or i in hbm else pltpu.VMEM
         placed.append(pltpu.with_memory_space_constraint(arg, held))
     return pl.pallas_call(
         kernel,
         name=name,
         out_shape=[
-            jax.ShapeDtypeStruct(shape, dtype) if i in out_hbm else pltpu.VMEM(shape, dtype)
+            pltpu.HBM(shape, dtype) if i in out_plain or i in out_hbm else pltpu.VMEM(shape, dtype)
             for i, (shape, dtype) in enumerate(outs)
         ],
         in_specs=specs,
-        out_specs=[whole] * len(outs),
+        out_specs=[
+            pl.BlockSpec(memory_space=pl.ANY if i in out_hbm else pltpu.VMEM) for i in range(len(outs))
+        ],
         scratch_shapes=list(scratch),
         compiler_params=pltpu.CompilerParams(vmem_limit_bytes=VMEM_LIMIT),
     )(*placed)
@@ -353,6 +376,8 @@
     )
     own = ((width, cap), F32)
     block = ((tiles, sh.rows, LANES), BF16)
+    groups = noff // GROUP
+    lattice_shape = (groups, width, GROUP * width)
     start, rank, send = call(
         functools.partial(first_kernel, sh),
         "first",
@@ -363,18 +388,21 @@
         scratch=[pltpu.VMEM((3, tiles, cap), F32)],
     )
     recv = exchange(send)
-    pairs, flipped, turned = call(
+    pairs, turned, flipped = call(
         functools.partial(tables_kernel, sh),
         "tables",
-        [((noff, cap, cap), BF16), ((width, noff * width), BF16), ((width, width), BF16)],
+        [((noff, cap, cap), BF16), ((width, width), BF16), (lattice_shape, BF16)],
         [mine, counts, local_target.T, local_offset.T, tmatrix, lattice],
         smem=2,
         plain=True,
         hbm=(5,),
+        out_hbm=(2,),
         scratch=[
-            pltpu.VMEM((sh.nl, cap), jnp.int32),
+            pltpu.VMEM((sh.nl, cap, cap), BF16),
             pltpu.VMEM((noff, width, width), BF16),
-            pltpu.SemaphoreType.DMA((noff // GROUP,)),
+            pltpu.VMEM(lattice_shape, BF16),
+            pltpu.SemaphoreType.DMA((groups,)),
+            pltpu.SemaphoreType.DMA((groups,)),
         ],
     )
     current, olds, copies, keys, seen = start, [], [], [], []
@@ -386,13 +414,16 @@
             outs.append(((width, sh.inbound), F32))
         if step == 0:
             outs.append(((sh.inbound, LANES), BF16))
+            outs.append((lattice_shape, BF16))
         result = call(
             functools.partial(step_kernel, sh, step),
             f"step{step}",
             outs,
             [mine, counts, recv, rank, pairs, turned, flipped, current, *olds, *copies, *keys],
             smem=2,
-            scratch=[pltpu.VMEM((width, sh.sources), BF16)],
+            hbm=() if step else (6,),
+            scratch=[pltpu.VMEM((width, sh.sources), BF16)]
+            + ([] if step else [pltpu.SemaphoreType.DMA((groups,))]),
         )
         vector, current, sums, send = result[:4]
         olds.append(vector)
@@ -400,14 +431,14 @@
         if not last:
             copies.append(result[4])
         if step == 0:
-            keys = [result[5]]
+            keys, flipped = [result[5]], result[6]
         recv = exchange(send)
     basis, hess = call(
         functools.partial(last_kernel, sh),
         "last",
         [((ITERS + 1, width, cap), F32), ((ITERS + 1, ITERS), F32)],
         [recv, *seen, *olds, current],
-        out_hbm=(0, 1),
+        out_plain=(0, 1),
     )
     return jnp.transpose(basis, (0, 2, 1)), hess
 

time: 116 us -> 113 us (0.974)
  local copies, waits for them, and re-layouts: 5.59 us -> 0 us
  Pallas kernels: 44 us -> 46.5 us
    unnamed x6 -> x0, local copies, waits for them, and re-layouts: 5.59 us -> none
    pallas_call x6, Pallas kernels: 44 us -> 46.5 us  [call(): pl.pallas_call(kernel, name=name, out_shape=[pltpu.HBM(shape, dtype) if i...]
  transfers between devices with their start and end apart: 1 -> 1, of which waited for: 0 -> 1; matrix products, arithmetic and copies ran while one was open for 0% -> 0% of each run, Pallas kernels for 14% -> 15%
where the time goes in v5:
time: 113 us; the launch traced here: 112 us
  blocking collectives  57.1 us (51%)
  Pallas kernels  46.5 us (41%)
  starting transfers between devices  7.36 us (7%)
    all_to_all x3, blocking collectives, per_device(): recv = exchange(send)  57.1 us
    pallas_call x6, Pallas kernels, call(): pl.pallas_call(kernel, name=name, out_shape=[pltpu.HBM(shape, dtype) if i...  46.5 us
    all_to_all x1, starting transfers between devices, per_device(): recv = exchange(send)  7.36 us
  transfers between devices with their start and end apart: 1, of which 1 were waited for; matrix products, arithmetic and copies ran while one was open for 0% of the time, Pallas kernels for 15%

profile of v5, /device:TPU:0, one launch (start us, length us, event | category | flops | bytes accessed | tf_op | source)
XLA Modules:
  0.0 112.4 jit_solution(15988339510779543787)
XLA Ops:
  0.6 2.7 %first.1 = (f32[320,128]{1,0:T(8,128)S(1)}, s32[16,128]{1,0:T(8,128)S(1)}, bf16[16,176,128]{2,1,0:T(8,128)(2,1)}) custom-call(s32[1]{0:T(128)} %bitcast.mine_ref.refs_0_, s32[16]{0:T(128)} %refs_1_.5, f32[320,128]{1,0:T(8,128)} %bitcast.8, s32[4,128]{1,0:T(4,128)} %bitcast.11, s32[4,128]{1,0:T(4,128)} %bitcast.12, s32[4,128]{1,0:T(4,128)} %bitcast.13), custom_call_target="tpu_custom_call" | custom-call | tf_op jit(solution)/shard_map/first/pallas_call | solution.py:342
  3.4 7.4 %all-to-all-start = ((bf16[16,176,128]{2,1,0:T(8,128)(2,1)}), bf16[16,176,128]{2,1,0:T(8,128)(2,1)S(1)}, u32[]{:S(2)}, u32[]{:S(2)}) async-start(bf16[16,176,128]{2,1,0:T(8,128)(2,1)} %get-tuple-element.26), calls=%async_computation | async-start | bytes 1441792 | tf_op jit(solution)/shard_map/all_to_all | solution.py:390
  10.7 16.9 %tables.1 = (bf16[32,128,128]{2,1,0:T(8,128)(2,1)S(1)}, bf16[320,320]{1,0:T(8,128)(2,1)S(1)}, bf16[8,320,1280]{2,1,0:T(8,128)(2,1)}) custom-call(s32[1]{0:T(128)} %bitcast.mine_ref.refs_0_, s32[16]{0:T(128)} %refs_1_.5, s32[24,128]{1,0:T(8,128)} %bitcast.9, s32[24,128]{1,0:T(8,128)} %bitcast.10, bf16[320,320]{1,0:T(8,128)(2,1)} %tmatrix_ref.1, ...), custom_call_target="tpu_custom_call" | custom-call | tf_op jit(solution)/shard_map/tables/pallas_call | solution.py:342
  27.6 0.8 all-to-all-done.refs_2_
  28.4 10.4 %step0.1 = (f32[320,128]{1,0:T(8,128)S(1)}, f32[320,128]{1,0:T(8,128)S(1)}, f32[8,128]{1,0:T(8,128)S(1)}, bf16[16,176,128]{2,1,0:T(8,128)(2,1)S(1)}, f32[320,102...) custom-call(s32[1]{0:T(128)} %bitcast.mine_ref.refs_0_, s32[16]{0:T(128)} %refs_1_.5, ...), custom_call_target="tpu_custom_call" | custom-call | tf_op jit(solution)/shard_map/step0/pallas_call | solution.py:342
  38.8 24.2 %all_to_all.20.refs_2_ = bf16[16,176,128]{2,1,0:T(8,128)(2,1)S(1)} all-to-all(bf16[16,176,128]{2,1,0:T(8,128)(2,1)S(1)} %get-tuple-element.32), channel_id=1, replica_groups=mesh['groups'=2,'tile'=16] {'tile'}, dimensions={0} | all-to-all | bytes 1441792 | tf_op jit(solution)/shard_map/all_to_all | solution.py:435
  62.9 8.0 %step1.1 = (f32[320,128]{1,0:T(8,128)S(1)}, f32[320,128]{1,0:T(8,128)S(1)}, f32[8,128]{1,0:T(8,128)S(1)}, bf16[16,176,128]{2,1,0:T(8,128)(2,1)S(1)}, f32[320,1024]{1,0:T(8,128)S(1)}) custom-call(s32[1]{0:T(128)} %bitcast.mine_ref.refs_0_, s32[16]{0:T(128)} %refs_1_.5, bf16[16,176,128]{2,1,0:T(8,128)(2,1)S(1)} %all_to_all.20.refs_2_, ...), custom_call_target="tpu_custom_call" | custom-call | tf_op jit(solution)/shard_map/step1/pallas_call | solution.py:342
  70.9 22.6 %all_to_all.21.refs_2_ = bf16[16,176,128]{2,1,0:T(8,128)(2,1)S(1)} all-to-all(bf16[16,176,128]{2,1,0:T(8,128)(2,1)S(1)} %get-tuple-element.38), channel_id=1, replica_groups=mesh['groups'=2,'tile'=16] {'tile'}, dimensions={0} | all-to-all | bytes 1441792 | tf_op jit(solution)/shard_map/all_to_all | solution.py:435
  93.5 7.6 %step2.1 = (f32[320,128]{1,0:T(8,128)S(1)}, f32[320,128]{1,0:T(8,128)S(1)}, f32[8,128]{1,0:T(8,128)S(1)}, f32[16,8,128]{2,1,0:T(8,128)S(1)}) custom-call(s32[1]{0:T(128)} %bitcast.mine_ref.refs_0_, s32[16]{0:T(128)} %refs_1_.5, bf16[16,176,128]{2,1,0:T(8,128)(2,1)S(1)} %all_to_all.21.refs_2_, s32[16,128]{1,0:T(8,128)S(1)} %get-tuple-element.27.refs_3_, ...), custom_call_target="tpu_custom_call" | custom-call | tf_op jit(solution)/shard_map/step2/pallas_call | solution.py:342
  101.0 10.3 %all_to_all.22.recv_ref = f32[16,8,128]{2,1,0:T(8,128)S(1)} all-to-all(f32[16,8,128]{2,1,0:T(8,128)S(1)} %get-tuple-element.42), channel_id=1, replica_groups=mesh['groups'=2,'tile'=16] {'tile'}, dimensions={0} | all-to-all | bytes 131072 | tf_op jit(solution)/shard_map/all_to_all | solution.py:435
  111.4 1.0 last.1
Async XLA Ops:
  3.4 25.0 %all-to-all-start = ((bf16[16,176,128]{2,1,0:T(8,128)(2,1)}), bf16[16,176,128]{2,1,0:T(8,128)(2,1)S(1)}, u32[]{:S(2)}, u32[]{:S(2)}) async-start(bf16[16,176,128]{2,1,0:T(8,128)(2,1)} %get-tuple-element.26), calls=%async_computation | async-start | bytes 1441792 | tf_op jit(solution)/shard_map/all_to_all | solution.py:390

commit v6 on v5

--- a/solution.py
+++ b/solution.py
@@ -9,7 +9,7 @@
 
 ITERS = 3
 LANES = 128
-GROUP = 4
+GROUP = 8
 AHEAD = 2
 F32 = jnp.float32
 BF16 = jnp.bfloat16
@@ -72,14 +72,14 @@
         self.slots = max(16, self.send_cap)
         self.fold = LANES // self.slots
         self.part = width // self.fold
-        self.extra = -(-self.part // 16) * 16
-        self.rows = self.extra + 16
+        self.extra = -(-self.part // 8) * 8
+        self.rows = self.extra + 8
         self.chunks = tiles // self.fold
         self.inbound = self.chunks * LANES
         self.sources = cap + self.inbound
 
 
-def pack(sh, mine, values, rank_ref, out_ref):
+def pack(sh, mine, values, rank_ref, out_ref, extra):
     parts = [values[f * sh.part : (f + 1) * sh.part] for f in range(sh.fold)]
     wide = jnp.concatenate(parts, axis=1)
     lane = iota((LANES, sh.cap), 0)
@@ -87,21 +87,23 @@
 
     def body(d):
         rank = rank_ref[pl.ds(d, 1), :]
-        picked = jnp.concatenate([flag(rank + shift == lane) for shift in shifts], axis=1)
-        block = dot_nt(wide, picked).astype(BF16)
+        picked = [flag(rank + shift == lane) for shift in shifts]
+        block = [dot_nt(wide, jnp.concatenate(picked, axis=1))]
         if sh.extra > sh.part:
-            block = jnp.concatenate([block, jnp.zeros((sh.extra - sh.part, LANES), BF16)], axis=0)
-        out_ref[d, 0 : sh.extra, :] = block
+            block.append(jnp.zeros((sh.extra - sh.part, LANES), F32))
+        block.append(extra(d, picked[0]))
+        out_ref[d] = jnp.concatenate(block, axis=0).astype(BF16)
 
     each(sh.tiles, body)
 
 
 def sum_rows(sums):
-    row = iota((16, LANES), 0)
-    tile = jnp.zeros((16, LANES), F32)
+    row, col = iota((8, LANES), 0), iota((8, LANES), 1)
+    tile = jnp.zeros((8, LANES), F32)
     for q, value in enumerate(sums):
-        for p, piece in enumerate(pieces(value)):
-            tile = jnp.where(row == 4 + 3 * q + p, piece, tile)
+        first, second, third = pieces(value)
+        spread = jnp.where(col < 32, first, jnp.where(col < 64, second, third))
+        tile = jnp.where(row == 4 + q, spread, tile)
     return tile
 
 
@@ -129,21 +131,16 @@
     code_ref[0] = targets
     code_ref[1] = offsets
     code_ref[2] = named
-    pack(sh, mine, start.astype(BF16), rank_ref, out_ref)
     sums = sum_rows([total(start * start)])
-    shift = lax.rem(mine, sh.fold) * sh.slots
-    row = iota((16, LANES), 0)
-    lane = iota((LANES, sh.cap), 0)
-
-    def body(d):
-        picked = flag(rank_ref[pl.ds(d, 1), :] + shift == lane)
-        table = jnp.zeros((16, sh.cap), F32)
+    row = iota((8, LANES), 0)
+
+    def extra(d, picked):
+        table = jnp.zeros((8, sh.cap), F32)
         for q in range(3):
             table = jnp.where(row == q, code_ref[q, pl.ds(d, 1), :], table)
-        extra = dot_nt(table.astype(BF16), picked) + sums
-        out_ref[d, sh.extra :, :] = extra.astype(BF16)
-
-    each(sh.tiles, body)
+        return dot_nt(table.astype(BF16), picked) + sums
+
+    pack(sh, mine, start.astype(BF16), rank_ref, out_ref, extra)
 
 
 def slot_keys(sh, target, offset, empty):
@@ -233,22 +230,22 @@
         load.start()
     mine = mine_ref[0]
     count = counts_ref[mine]
-    extras = jnp.zeros((16, LANES), F32)
+    extras = jnp.zeros((8, LANES), F32)
     for s in range(sh.tiles):
-        extras = extras + recv_ref[s, sh.extra :, :].astype(F32)
+        extras = extras + recv_ref[s].astype(F32)[sh.extra :]
     sums = []
     for q in range(max(1, step + 1)):
-        r = 4 + 3 * q
-        sums.append(extras[r : r + 1, 0:1] + extras[r + 1 : r + 2, 0:1] + extras[r + 2 : r + 3, 0:1])
+        r = extras[4 + q : 5 + q]
+        sums.append(r[:, 0:1] + r[:, 32:33] + r[:, 64:65])
     vector = next_vector(step, current_ref[...], [ref[...] for ref in olds], sums)
     vector_out[...] = vector
     x_ref[:, 0 : sh.cap] = vector.astype(BF16)
     if step == 0:
         key_ref = key_out[0]
         for c in range(sh.chunks):
-            table = jnp.zeros((16, LANES), F32)
+            table = jnp.zeros((8, LANES), F32)
             for s in range(c * sh.fold, (c + 1) * sh.fold):
-                table = table + recv_ref[s, sh.extra :, :].astype(F32)
+                table = table + recv_ref[s].astype(F32)[sh.extra :]
             target = wrap(table[0:1].astype(jnp.int32), count).astype(F32)
             key_ref[c * LANES : (c + 1) * LANES, :] = slot_keys(sh, target, table[1:2], 1.0 - table[2:3])
     else:
@@ -257,9 +254,9 @@
     for c in range(sh.chunks):
         parts = []
         for f in range(sh.fold):
-            part = recv_ref[c * sh.fold, 0 : sh.extra, :].astype(F32)[: sh.part]
+            part = recv_ref[c * sh.fold].astype(F32)[: sh.part]
             for m in range(1, sh.fold):
-                other = recv_ref[c * sh.fold + m, 0 : sh.extra, :].astype(F32)[: sh.part]
+                other = recv_ref[c * sh.fold + m].astype(F32)[: sh.part]
                 part = jnp.where(lane_group == (m + f) % sh.fold, other, part)
             if f:
                 part = pltpu.roll(part, LANES - f * sh.slots, 1)
@@ -300,10 +297,8 @@
         for d in range(sh.tiles):
             send_out[d] = tile
     else:
-        pack(sh, mine, image.astype(BF16), rank_ref, send_out)
-        tile = sum_rows(out).astype(BF16)
-        for d in range(sh.tiles):
-            send_out[d, sh.extra :, :] = tile
+        tile = sum_rows(out)
+        pack(sh, mine, image.astype(BF16), rank_ref, send_out, lambda d, picked: tile)
 
 
 def last_kernel(sh, recv_ref, *refs):

time: 113 us -> 109 us (0.965)
  Pallas kernels: 46.5 us -> 43.6 us
  blocking collectives: 57.1 us -> 55.5 us
    pallas_call x6, Pallas kernels: 46.5 us -> 43.6 us  [call(): pl.pallas_call(kernel, name=name, out_shape=[pltpu.HBM(shape, dtype) if i...]
    all_to_all x3, blocking collectives: 57.1 us -> 55.5 us  [per_device(): recv = exchange(send)]
  transfers between devices with their start and end apart: 1 -> 1, of which waited for: 1 -> 1; matrix products, arithmetic and copies ran while one was open for 0% -> 0% of each run, Pallas kernels for 15% -> 14%
where the time goes in v6:
time: 109 us
  blocking collectives  55.5 us (51%)
  Pallas kernels  43.6 us (40%)
  starting transfers between devices  7.36 us (7%)
  waiting for transfers between devices  1.48 us (1%)
    all_to_all x3, blocking collectives, per_device(): recv = exchange(send)  55.5 us
    pallas_call x6, Pallas kernels, call(): pl.pallas_call(kernel, name=name, out_shape=[pltpu.HBM(shape, dtype) if i...  43.6 us
    all_to_all x1, starting transfers between devices, per_device(): recv = exchange(send)  7.36 us
  transfers between devices with their start and end apart: 1, of which 1 were waited for; matrix products, arithmetic and copies ran while one was open for 0% of the time, Pallas kernels for 14%

profile of v6, /device:TPU:0, one launch (start us, length us, event | category | flops | bytes accessed | tf_op | source)
XLA Modules:
  0.0 108.5 jit_solution(7787658730448558055)
XLA Ops:
  0.6 2.8 %first.1 = (f32[320,128]{1,0:T(8,128)S(1)}, s32[16,128]{1,0:T(8,128)S(1)}, bf16[16,168,128]{2,1,0:T(8,128)(2,1)}) custom-call(s32[1]{0:T(128)} %bitcast.mine_ref.refs_0_, s32[16]{0:T(128)} %refs_1_.5, f32[320,128]{1,0:T(8,128)} %bitcast.8, s32[4,128]{1,0:T(4,128)} %bitcast.11, s32[4,128]{1,0:T(4,128)} %bitcast.12, s32[4,128]{1,0:T(4,128)} %bitcast.13), custom_call_target="tpu_custom_call" | custom-call | tf_op jit(solution)/shard_map/first/pallas_call | solution.py:337
  3.4 7.4 %all-to-all-start = ((bf16[16,168,128]{2,1,0:T(8,128)(2,1)}), bf16[16,168,128]{2,1,0:T(8,128)(2,1)S(1)}, u32[]{:S(2)}, u32[]{:S(2)}) async-start(bf16[16,168,128]{2,1,0:T(8,128)(2,1)} %get-tuple-element.26), calls=%async_computation | async-start | bytes 1376256 | tf_op jit(solution)/shard_map/all_to_all | solution.py:385
  10.8 15.6 %tables.1 = (bf16[32,128,128]{2,1,0:T(8,128)(2,1)S(1)}, bf16[320,320]{1,0:T(8,128)(2,1)S(1)}, bf16[4,320,2560]{2,1,0:T(8,128)(2,1)}) custom-call(s32[1]{0:T(128)} %bitcast.mine_ref.refs_0_, s32[16]{0:T(128)} %refs_1_.5, s32[24,128]{1,0:T(8,128)} %bitcast.9, s32[24,128]{1,0:T(8,128)} %bitcast.10, bf16[320,320]{1,0:T(8,128)(2,1)} %tmatrix_ref.1, ...), custom_call_target="tpu_custom_call" | custom-call | tf_op jit(solution)/shard_map/tables/pallas_call | solution.py:337
  26.4 1.5 %all-to-all-done.refs_2_ = bf16[16,168,128]{2,1,0:T(8,128)(2,1)S(1)} async-done(((bf16[16,168,128]{2,1,0:T(8,128)(2,1)}), bf16[16,168,128]{2,1,0:T(8,128)(2,1)S(1)}, u32[]{:S(2)}, u32[]{:S(2)}) %all-to-all-start) | async-done | bytes 688160 | tf_op jit(solution)/shard_map/all_to_all | solution.py:385
  27.9 8.7 %step0.1 = (f32[320,128]{1,0:T(8,128)S(1)}, f32[320,128]{1,0:T(8,128)S(1)}, f32[8,128]{1,0:T(8,128)S(1)}, bf16[16,168,128]{2,1,0:T(8,128)(2,1)S(1)}, f32[320,102...) custom-call(s32[1]{0:T(128)} %bitcast.mine_ref.refs_0_, s32[16]{0:T(128)} %refs_1_.5, ...), custom_call_target="tpu_custom_call" | custom-call | tf_op jit(solution)/shard_map/step0/pallas_call | solution.py:337
  36.5 23.4 %all_to_all.20.refs_2_ = bf16[16,168,128]{2,1,0:T(8,128)(2,1)S(1)} all-to-all(bf16[16,168,128]{2,1,0:T(8,128)(2,1)S(1)} %get-tuple-element.32), channel_id=1, replica_groups=mesh['groups'=2,'tile'=16] {'tile'}, dimensions={0} | all-to-all | bytes 1376256 | tf_op jit(solution)/shard_map/all_to_all | solution.py:430
  59.9 8.0 %step1.1 = (f32[320,128]{1,0:T(8,128)S(1)}, f32[320,128]{1,0:T(8,128)S(1)}, f32[8,128]{1,0:T(8,128)S(1)}, bf16[16,168,128]{2,1,0:T(8,128)(2,1)S(1)}, f32[320,1024]{1,0:T(8,128)S(1)}) custom-call(s32[1]{0:T(128)} %bitcast.mine_ref.refs_0_, s32[16]{0:T(128)} %refs_1_.5, bf16[16,168,128]{2,1,0:T(8,128)(2,1)S(1)} %all_to_all.20.refs_2_, ...), custom_call_target="tpu_custom_call" | custom-call | tf_op jit(solution)/shard_map/step1/pallas_call | solution.py:337
  67.9 21.9 %all_to_all.21.refs_2_ = bf16[16,168,128]{2,1,0:T(8,128)(2,1)S(1)} all-to-all(bf16[16,168,128]{2,1,0:T(8,128)(2,1)S(1)} %get-tuple-element.38), channel_id=1, replica_groups=mesh['groups'=2,'tile'=16] {'tile'}, dimensions={0} | all-to-all | bytes 1376256 | tf_op jit(solution)/shard_map/all_to_all | solution.py:430
  89.9 7.5 %step2.1 = (f32[320,128]{1,0:T(8,128)S(1)}, f32[320,128]{1,0:T(8,128)S(1)}, f32[8,128]{1,0:T(8,128)S(1)}, f32[16,8,128]{2,1,0:T(8,128)S(1)}) custom-call(s32[1]{0:T(128)} %bitcast.mine_ref.refs_0_, s32[16]{0:T(128)} %refs_1_.5, bf16[16,168,128]{2,1,0:T(8,128)(2,1)S(1)} %all_to_all.21.refs_2_, s32[16,128]{1,0:T(8,128)S(1)} %get-tuple-element.27.refs_3_, ...), custom_call_target="tpu_custom_call" | custom-call | tf_op jit(solution)/shard_map/step2/pallas_call | solution.py:337
  97.4 10.2 %all_to_all.22.recv_ref = f32[16,8,128]{2,1,0:T(8,128)S(1)} all-to-all(f32[16,8,128]{2,1,0:T(8,128)S(1)} %get-tuple-element.42), channel_id=1, replica_groups=mesh['groups'=2,'tile'=16] {'tile'}, dimensions={0} | all-to-all | bytes 131072 | tf_op jit(solution)/shard_map/all_to_all | solution.py:430
  107.5 1.0 last.1
Async XLA Ops:
  3.4 24.5 %all-to-all-start = ((bf16[16,168,128]{2,1,0:T(8,128)(2,1)}), bf16[16,168,128]{2,1,0:T(8,128)(2,1)S(1)}, u32[]{:S(2)}, u32[]{:S(2)}) async-start(bf16[16,168,128]{2,1,0:T(8,128)(2,1)} %get-tuple-element.26), calls=%async_computation | async-start | bytes 1376256 | tf_op jit(solution)/shard_map/all_to_all | solution.py:385

commit v7 on v6

--- a/solution.py
+++ b/solution.py
@@ -11,6 +11,7 @@
 LANES = 128
 GROUP = 8
 AHEAD = 2
+BLOCKS = 2
 F32 = jnp.float32
 BF16 = jnp.bfloat16
 VMEM_LIMIT = 28 * 1024 * 1024
@@ -85,16 +86,21 @@
     lane = iota((LANES, sh.cap), 0)
     shifts = [lax.rem(mine + f, sh.fold) * sh.slots for f in range(sh.fold)]
 
-    def body(d):
-        rank = rank_ref[pl.ds(d, 1), :]
-        picked = [flag(rank + shift == lane) for shift in shifts]
-        block = [dot_nt(wide, jnp.concatenate(picked, axis=1))]
-        if sh.extra > sh.part:
-            block.append(jnp.zeros((sh.extra - sh.part, LANES), F32))
-        block.append(extra(d, picked[0]))
-        out_ref[d] = jnp.concatenate(block, axis=0).astype(BF16)
-
-    each(sh.tiles, body)
+    def body(e):
+        some = []
+        for d in range(BLOCKS):
+            rank = rank_ref[pl.ds(e * BLOCKS + d, 1), :]
+            some.append([flag(rank + shift == lane) for shift in shifts])
+        picked = jnp.concatenate([jnp.concatenate(one, axis=1) for one in some], axis=0)
+        blocks = dot_nt(wide, picked)
+        for d in range(BLOCKS):
+            block = [blocks[:, d * LANES : (d + 1) * LANES]]
+            if sh.extra > sh.part:
+                block.append(jnp.zeros((sh.extra - sh.part, LANES), F32))
+            block.append(extra(e * BLOCKS + d, some[d][0]))
+            out_ref[e * BLOCKS + d] = jnp.concatenate(block, axis=0).astype(BF16)
+
+    each(sh.tiles // BLOCKS, body)
 
 
 def sum_rows(sums):
@@ -291,9 +297,10 @@
         seen = jnp.where(row8 == q, value, seen)
     sums_out[...] = seen
     if last:
-        tile = jnp.zeros((8, LANES), F32)
+        col = iota((1, LANES), 1)
+        tile = jnp.zeros((1, LANES), F32)
         for q, value in enumerate(out):
-            tile = jnp.where(row8 == q, value, tile)
+            tile = jnp.where(col == q, value, tile)
         for d in range(sh.tiles):
             send_out[d] = tile
     else:
@@ -305,22 +312,22 @@
     seen = refs[:ITERS]
     vectors = refs[ITERS : 2 * ITERS]
     image_ref, basis_ref, hess_ref = refs[2 * ITERS :]
-    final = jnp.zeros((8, LANES), F32)
+    final = jnp.zeros((1, LANES), F32)
     for s in range(sh.tiles):
         final = final + recv_ref[s]
-    tables = [ref[...] for ref in seen[1:]] + [final]
+    sums = [final[:, q : q + 1] for q in range(ITERS + 1)]
+    tables = [[ref[q : q + 1, 0:1] for q in range(ITERS)] for ref in seen[1:]] + [sums]
     row = iota((ITERS + 1, ITERS), 0)
     col = iota((ITERS + 1, ITERS), 1)
     hess = jnp.zeros((ITERS + 1, ITERS), F32)
     for k in range(ITERS):
-        square = tables[k][k + 1 : k + 2, 0:1]
+        square = tables[k][k + 1]
         for j in range(k + 1):
-            product = tables[k][j : j + 1, 0:1]
+            product = tables[k][j]
             square = square - product * product
             hess = jnp.where((row == j) & (col == k), (1.0 if j == k else 0.0) - product, hess)
         hess = jnp.where((row == k + 1) & (col == k), jnp.sqrt(square), hess)
     hess_ref[...] = hess
-    sums = [final[q : q + 1, 0:1] for q in range(ITERS + 1)]
     olds = [ref[...] for ref in vectors]
     for j in range(ITERS):
         basis_ref[j] = olds[j]
@@ -404,7 +411,7 @@
     for step in range(ITERS):
         last = step == ITERS - 1
         outs = [own, own, ((8, LANES), F32)]
-        outs.append(((tiles, 8, LANES), F32) if last else block)
+        outs.append(((tiles, 1, LANES), F32) if last else block)
         if not last:
             outs.append(((width, sh.inbound), F32))
         if step == 0:

time: 109 us -> 109 us (level)
  no operation moved by 1% of the time
where the time goes in v7:
time: 109 us; the launch traced here: 108 us
  blocking collectives  55 us (50%)
  Pallas kernels  44 us (40%)
  starting transfers between devices  7.36 us (7%)
  waiting for transfers between devices  1.47 us (1%)
    all_to_all x3, blocking collectives, per_device(): recv = exchange(send)  55 us
    pallas_call x6, Pallas kernels, call(): pl.pallas_call(kernel, name=name, out_shape=[pltpu.HBM(shape, dtype) if i...  44 us
    all_to_all x1, starting transfers between devices, per_device(): recv = exchange(send)  7.36 us
  transfers between devices with their start and end apart: 1, of which 1 were waited for; matrix products, arithmetic and copies ran while one was open for 0% of the time, Pallas kernels for 14%

profile of v7, /device:TPU:0, one launch (start us, length us, event | category | flops | bytes accessed | tf_op | source)
XLA Modules:
  0.0 108.4 jit_solution(16141410614333909751)
XLA Ops:
  0.6 2.7 %first.1 = (f32[320,128]{1,0:T(8,128)S(1)}, s32[16,128]{1,0:T(8,128)S(1)}, bf16[16,168,128]{2,1,0:T(8,128)(2,1)}) custom-call(s32[1]{0:T(128)} %bitcast.mine_ref.refs_0_, s32[16]{0:T(128)} %refs_1_.5, f32[320,128]{1,0:T(8,128)} %bitcast.8, s32[4,128]{1,0:T(4,128)} %bitcast.11, s32[4,128]{1,0:T(4,128)} %bitcast.12, s32[4,128]{1,0:T(4,128)} %bitcast.13), custom_call_target="tpu_custom_call" | custom-call | tf_op jit(solution)/shard_map/first/pallas_call | solution.py:344
  3.3 7.4 %all-to-all-start = ((bf16[16,168,128]{2,1,0:T(8,128)(2,1)}), bf16[16,168,128]{2,1,0:T(8,128)(2,1)S(1)}, u32[]{:S(2)}, u32[]{:S(2)}) async-start(bf16[16,168,128]{2,1,0:T(8,128)(2,1)} %get-tuple-element.26), calls=%async_computation | async-start | bytes 1376256 | tf_op jit(solution)/shard_map/all_to_all | solution.py:392
  10.7 15.6 %tables.1 = (bf16[32,128,128]{2,1,0:T(8,128)(2,1)S(1)}, bf16[320,320]{1,0:T(8,128)(2,1)S(1)}, bf16[4,320,2560]{2,1,0:T(8,128)(2,1)}) custom-call(s32[1]{0:T(128)} %bitcast.mine_ref.refs_0_, s32[16]{0:T(128)} %refs_1_.5, s32[24,128]{1,0:T(8,128)} %bitcast.9, s32[24,128]{1,0:T(8,128)} %bitcast.10, bf16[320,320]{1,0:T(8,128)(2,1)} %tmatrix_ref.1, ...), custom_call_target="tpu_custom_call" | custom-call | tf_op jit(solution)/shard_map/tables/pallas_call | solution.py:344
  26.4 1.5 %all-to-all-done.refs_2_ = bf16[16,168,128]{2,1,0:T(8,128)(2,1)S(1)} async-done(((bf16[16,168,128]{2,1,0:T(8,128)(2,1)}), bf16[16,168,128]{2,1,0:T(8,128)(2,1)S(1)}, u32[]{:S(2)}, u32[]{:S(2)}) %all-to-all-start) | async-done | bytes 688160 | tf_op jit(solution)/shard_map/all_to_all | solution.py:392
  27.8 9.1 %step0.1 = (f32[320,128]{1,0:T(8,128)S(1)}, f32[320,128]{1,0:T(8,128)S(1)}, f32[8,128]{1,0:T(8,128)S(1)}, bf16[16,168,128]{2,1,0:T(8,128)(2,1)S(1)}, f32[320,102...) custom-call(s32[1]{0:T(128)} %bitcast.mine_ref.refs_0_, s32[16]{0:T(128)} %refs_1_.5, ...), custom_call_target="tpu_custom_call" | custom-call | tf_op jit(solution)/shard_map/step0/pallas_call | solution.py:344
  37.0 23.4 %all_to_all.20.refs_2_ = bf16[16,168,128]{2,1,0:T(8,128)(2,1)S(1)} all-to-all(bf16[16,168,128]{2,1,0:T(8,128)(2,1)S(1)} %get-tuple-element.32), channel_id=1, replica_groups=mesh['groups'=2,'tile'=16] {'tile'}, dimensions={0} | all-to-all | bytes 1376256 | tf_op jit(solution)/shard_map/all_to_all | solution.py:437
  60.3 8.0 %step1.1 = (f32[320,128]{1,0:T(8,128)S(1)}, f32[320,128]{1,0:T(8,128)S(1)}, f32[8,128]{1,0:T(8,128)S(1)}, bf16[16,168,128]{2,1,0:T(8,128)(2,1)S(1)}, f32[320,1024]{1,0:T(8,128)S(1)}) custom-call(s32[1]{0:T(128)} %bitcast.mine_ref.refs_0_, s32[16]{0:T(128)} %refs_1_.5, bf16[16,168,128]{2,1,0:T(8,128)(2,1)S(1)} %all_to_all.20.refs_2_, ...), custom_call_target="tpu_custom_call" | custom-call | tf_op jit(solution)/shard_map/step1/pallas_call | solution.py:344
  68.3 21.9 %all_to_all.21.refs_2_ = bf16[16,168,128]{2,1,0:T(8,128)(2,1)S(1)} all-to-all(bf16[16,168,128]{2,1,0:T(8,128)(2,1)S(1)} %get-tuple-element.38), channel_id=1, replica_groups=mesh['groups'=2,'tile'=16] {'tile'}, dimensions={0} | all-to-all | bytes 1376256 | tf_op jit(solution)/shard_map/all_to_all | solution.py:437
  90.2 7.5 %step2.1 = (f32[320,128]{1,0:T(8,128)S(1)}, f32[320,128]{1,0:T(8,128)S(1)}, f32[8,128]{1,0:T(8,128)S(1)}, f32[16,1,128]{2,1,0:T(1,128)S(1)}) custom-call(s32[1]{0:T(128)} %bitcast.mine_ref.refs_0_, s32[16]{0:T(128)} %refs_1_.5, bf16[16,168,128]{2,1,0:T(8,128)(2,1)S(1)} %all_to_all.21.refs_2_, s32[16,128]{1,0:T(8,128)S(1)} %get-tuple-element.27.refs_3_, ...), custom_call_target="tpu_custom_call" | custom-call | tf_op jit(solution)/shard_map/step2/pallas_call | solution.py:344
  97.7 9.7 %all_to_all.22.recv_ref = f32[16,1,128]{2,1,0:T(1,128)S(1)} all-to-all(f32[16,1,128]{2,1,0:T(1,128)S(1)} %get-tuple-element.42), channel_id=1, replica_groups=mesh['groups'=2,'tile'=16] {'tile'}, dimensions={0} | all-to-all | bytes 16384 | tf_op jit(solution)/shard_map/all_to_all | solution.py:437
  107.4 1.0 last.1
Async XLA Ops:
  3.3 24.5 %all-to-all-start = ((bf16[16,168,128]{2,1,0:T(8,128)(2,1)}), bf16[16,168,128]{2,1,0:T(8,128)(2,1)S(1)}, u32[]{:S(2)}, u32[]{:S(2)}) async-start(bf16[16,168,128]{2,1,0:T(8,128)(2,1)} %get-tuple-element.26), calls=%async_computation | async-start | bytes 1376256 | tf_op jit(solution)/shard_map/all_to_all | solution.py:392
